TPU v7x, 32 devices: a whole 2x2x4 slice. The times are simulated.
32 devices in a mesh: feat: 8 (over z, core), row: 2 (over y), rep: 2 (over x).
Axes of the slice: x: 2, y: 2, z: 4, core: 2. Of those that a mesh axis runs over, the one named last changes fastest.
Arguments:
- activations: bfloat16 [32, 4608], P('feat', ('row', 'rep')), may hold values from -6 to 6
- enc_weight: bfloat16 [4608, 65536], P(('row', 'rep'), 'feat'), may hold values from -0.09375 to 0.09375
- enc_bias: float32 [65536], P('feat'), may hold values from -3 to 3
- dec_weight: bfloat16 [65536, 4608], P('feat', ('row', 'rep')), may hold values from -0.0234375 to 0.0234375
- dec_bias: float32 [4608], P(('row', 'rep')), may hold values from -3 to 3
- first_moment: bfloat16 [65536, 4608], P('feat', ('row', 'rep')), may hold values from -0.059814453 to 0.059814453
- second_moment: bfloat16 [65536, 4608], P('feat', ('row', 'rep')), may hold values from 9.953976e-06 to 0.0009994507
Outputs:
- reconstruction: bfloat16 [32, 4608], P('feat', ('row', 'rep'))
- dec_step: bfloat16 [65536, 4608], P('feat', ('row', 'rep'))
All inputs are finite; a program needn't handle non-finite values.
Results may differ from a plain program's by a relative error of at most 0.0053.
Values may be sent and summed in bfloat16 or wider, within the bound.
No kernel may reach another device: no remote copies, remote signals or barrier semaphores. Data moves between devices by JAX's collectives and lax.ppermute only.
A program may use at most 128 MiB of HBM per device.

v0:
```python
import jax
import jax.numpy as jnp
from jax import lax
from jax.sharding import PartitionSpec as P

sparsity_coef = 5.0
beta_one = 0.9
beta_two = 0.999
bias_one = 0.99997344
bias_two = 0.095207853
adam_eps = 1e-08
norm_eps = 1e-06


def shards(activations, enc_weight, enc_bias, dec_weight, dec_bias, first_moment, second_moment):
    local_rows = activations.shape[0]
    total_rows = local_rows * lax.axis_size("feat")
    centered = (activations.astype(jnp.float32) - dec_bias).astype(jnp.bfloat16)
    partial_value = jnp.dot(
        lax.all_gather(centered, "feat", axis=0, tiled=True),
        enc_weight,
        preferred_element_type=jnp.float32,
    )
    wide = dec_weight.astype(jnp.float32)
    squares = jnp.sum(wide * wide, axis=1)
    pre_sum, sum_squares = lax.psum((partial_value, squares), ("row", "rep"))
    active = jnp.maximum(pre_sum + enc_bias, 0.0).astype(jnp.bfloat16)
    rebuilt = (
        lax.psum_scatter(
            jnp.dot(active, dec_weight, preferred_element_type=jnp.float32),
            "feat",
            scatter_dimension=0,
            tiled=True,
        )
        + dec_bias
    )
    residual = (rebuilt - activations.astype(jnp.float32)).astype(jnp.bfloat16)
    all_residual = lax.all_gather(residual, "feat", axis=0, tiled=True)
    product = lax.dot_general(
        active, all_residual, (((0,), (0,)), ((), ())), preferred_element_type=jnp.float32
    )
    counts = jnp.sum(active.astype(jnp.float32), axis=0)
    row_norm = jnp.sqrt(sum_squares + norm_eps)
    gradient = (
        2.0 / total_rows * product
        + sparsity_coef / total_rows * counts[:, None] * wide / row_norm[:, None]
    )
    moment_one = beta_one * first_moment.astype(jnp.float32) + (1.0 - beta_one) * gradient
    moment_two = (
        beta_two * second_moment.astype(jnp.float32) + (1.0 - beta_two) * gradient * gradient
    )
    dec_step = (moment_one / bias_one / (jnp.sqrt(moment_two / bias_two) + adam_eps)).astype(
        jnp.bfloat16
    )
    return (rebuilt.astype(jnp.bfloat16), dec_step)


def solution(mesh):
    return jax.shard_map(
        shards,
        mesh=mesh,
        in_specs=(
            P("feat", ("row", "rep")),
            P(("row", "rep"), "feat"),
            P("feat"),
            P("feat", ("row", "rep")),
            P(("row", "rep")),
            P("feat", ("row", "rep")),
            P("feat", ("row", "rep")),
        ),
        out_specs=(P("feat", ("row", "rep")), P("feat", ("row", "rep"))),
        check_vma=False,
    )
```

profile of v0, /device:TPU:0, one launch (start us, length us, event | category | flops | bytes accessed | tf_op | source)
XLA Modules:
  0.0 216.2 jit_solution(7252405581490592939)
XLA Ops:
  7.2 0.0 copy-start.3
  7.2 0.0 all-reduce.4.cloned.1.call-start
  7.2 0.7 fusion.13
  7.9 15.7 %all-gather = bf16[8,4,1152]{2,1,0:T(4,128)(2,1)S(1)} all-gather(bf16[1,4,1152]{2,1,0:T(4,128)(2,1)S(1)} %fusion.13), channel_id=1, replica_groups=mesh['feat'=8,'row'=2,'rep'=2] {'feat'}, dimensions={0}, use_global_device_ids=true | all-gather | bytes 82944 | tf_op jit(solution)/shard_map/all_gather | solution.py:20
  23.6 0.0 copy-start.1
  23.6 10.7 %fusion.14 = f32[32,8192]{1,0:T(8,128)} fusion(bf16[32,1152]{1,0:T(8,128)(2,1)S(1)} %reshape.12, bf16[1152,8192]{1,0:T(8,128)(2,1)} %param.8), kind=kOutput, calls=%fused_computation.24 | convolution fusion | flops 603979776 | bytes 19996672 | tf_op jit(solution)/shard_map/dot_general | solution.py:19
  34.3 0.0 all-reduce.4.cloned.1.call-update
  34.4 0.0 all-reduce.6.cloned.1.call-start
  34.4 0.0 copy-done.3
  34.4 0.6 dynamic-slice
  35.7 14.0 %fusion.2 = f32[8192]{0:T(1024)S(1)} fusion(bf16[8192,1152]{1,0:T(8,128)(2,1)} %param.10), kind=kLoop, calls=%fused_computation.5 | loop fusion | flops 28303360 | bytes 18907136 | tf_op jit(solution)/shard_map/reduce_sum | solution.py:25
  49.7 0.0 copy-start
  49.7 0.0 copy-start.2
  49.7 16.4 %psum.15 = f32[8192]{0:T(1024)S(1)} all-reduce(f32[8192]{0:T(1024)S(1)} %fusion.2), channel_id=1, replica_groups=mesh['feat'=8,'row'=2,'rep'=2] {'row','rep'}, use_global_device_ids=true, to_apply=%region_4.0 | all-reduce | flops 8192 | bytes 65536 | tf_op jit(solution)/shard_map/psum | solution.py:26
  66.1 22.3 %all-reduce.4.cloned.1.call-done = f32[32,8192]{1,0:T(8,128)} async-done(((f32[32,8192]{1,0:T(8,128)}), f32[32,8192]{1,0:T(8,128)}) %all-reduce.4.cloned.1.call-update) | async-done | bytes 1048592 | tf_op jit(solution)/shard_map/psum | solution.py:26
  88.4 0.0 copy-done.1
  88.4 1.4 convert_reduce_fusion
  89.8 8.7 %fusion.15 = f32[32,1152]{1,0:T(8,128)} fusion(bf16[32,8192]{1,0:T(8,128)(2,1)S(1)} %get-tuple-element.3, bf16[8192,1152]{1,0:T(8,128)(2,1)} %param.10), kind=kOutput, calls=%fused_computation.25 | convolution fusion | flops 603979776 | bytes 19546112 | tf_op jit(solution)/shard_map/dot_general | solution.py:30
  98.5 0.0 all-reduce.6.cloned.1.call-update
  98.5 52.2 %all-reduce.6.cloned.1.call-done = f32[32,1152]{1,0:T(8,128)} async-done(((f32[32,1152]{1,0:T(8,128)}), f32[32,1152]{1,0:T(8,128)}) %all-reduce.6.cloned.1.call-update) | async-done | bytes 147472
  150.7 0.0 copy-done
  150.7 1.4 fusion.12
  152.1 15.5 %all-gather.1 = bf16[8,4,1152]{2,1,0:T(4,128)(2,1)S(1)} all-gather(bf16[1,4,1152]{2,1,0:T(4,128)(2,1)S(1)} %get-tuple-element.4), channel_id=1, replica_groups=mesh['feat'=8,'row'=2,'rep'=2] {'feat'}, dimensions={0}, use_global_device_ids=true | all-gather | bytes 82944 | tf_op jit(solution)/shard_map/all_gather | solution.py:38
  167.7 41.7 %fusion.8 = bf16[8192,1152]{1,0:T(8,128)(2,1)} fusion(bf16[8192,1152]{1,0:T(8,128)(2,1)} %param.13, bf16[8192,1152]{1,0:T(8,128)(2,1)} %param.10, bf16[8192,1152]{1,0:T(8,128)(2,1)} %param.12, bf16[32,8192]{1,0:T(8,128)(2,1)S(1)} %get-tuple-element.3, bf16[32,1152]{1,0:T(8,128)(2,1)S(1)} %reshape.14, f32[8192]{0:T(1024)S(1)} %add_sqrt_fusion, ...), kind=kOutput, calls=%fused_computation.11 | convolution fusion | flops 783286272 | bytes 76161024 | tf_op jit(solution)/shard_map/dot_general | solution.py:39
  (5 shorter events, 0.1 us)
Async XLA Ops:
  7.2 27.2 %copy-start.3 = (u32[32]{0:T(128)S(1)}, u32[32]{0:T(128)}, u32[]{:S(2)}) copy-start(u32[32]{0:T(128)} %constant.28) | copy-start | bytes 388
  7.2 81.2 %all-reduce.4.cloned.1.call-start = ((), (), s32[]{:S(2)}) async-start(), calls=%async_computation | async-start | bytes 2097152 | tf_op jit(solution)/shard_map/psum | solution.py:26
  23.6 64.8 %copy-start.1 = (f32[8192]{0:T(1024)S(1)}, f32[8192]{0:T(1024)}, u32[]{:S(2)}) copy-start(f32[8192]{0:T(1024)} %param.9) | copy-start | bytes 98308
  34.4 116.4 %all-reduce.6.cloned.1.call-start = ((), (), s32[]{:S(2)}) async-start(), calls=%async_computation.1 | async-start | bytes 294912
  49.7 101.1 %copy-start = (bf16[4,1152]{1,0:T(4,128)(2,1)S(1)}, bf16[4,1152]{1,0:T(4,128)(2,1)}, u32[]{:S(2)}) copy-start(bf16[4,1152]{1,0:T(4,128)(2,1)} %param.7) | copy-start | bytes 27652
  49.7 101.1 %copy-start.2 = (f32[1152]{0:T(1024)S(1)}, f32[1152]{0:T(1024)}, u32[]{:S(2)}) copy-start(f32[1152]{0:T(1024)} %param.11) | copy-start | bytes 13828
Sparse Core Ops, SparseCore 0:
  34.5 53.8 all-reduce.3
  98.6 52.0 all-reduce.5
where the time goes:
time: 217 us; the launch traced here: 216 us
  waiting for transfers between devices  74.6 us (34%)
  matrix products  61 us (28%)
  blocking collectives  47.6 us (22%)
  other arithmetic  17.5 us (8%)
  between operations  14.8 us (7%)
    unnamed x3, waiting for transfers between devices  52.3 us
    dot_general x1, matrix products, shards(): lax.dot_general(active, all_residual, (((0,), (0,)), ((), ())), preferred...  41.7 us
    psum x1, waiting for transfers between devices, shards(): pre_sum, sum_squares = lax.psum((partial_value, squares), ('row', 'rep'))  22.3 us
    psum x1, blocking collectives, shards(): pre_sum, sum_squares = lax.psum((partial_value, squares), ('row', 'rep'))  16.4 us
    all_gather x1, blocking collectives, shards(): lax.all_gather(centered, 'feat', axis=0, tiled=True)  15.7 us
    all_gather x1, blocking collectives, shards(): all_residual = lax.all_gather(residual, 'feat', axis=0, tiled=True)  15.5 us
    reduce_sum x1, other arithmetic, shards(): squares = jnp.sum(wide * wide, axis=1)  14 us
    dot_general x1, matrix products, shards(): jnp.dot(lax.all_gather(centered, 'feat', axis=0, tiled=True), enc_weight,...  10.7 us
  transfers between devices with their start and end apart: 2, of which 2 were waited for; matrix products, arithmetic and copies ran while one was open for 7% of the time, Pallas kernels for 0%

commit v1 on v0

v1 whole, which is shorter than its diff:
```python
import functools

import jax
import jax.experimental.pallas as pl
import jax.experimental.pallas.tpu as pltpu
import jax.numpy as jnp
from jax import lax
from jax.sharding import PartitionSpec as P

sparsity_coef = 5.0
beta_one = 0.9
beta_two = 0.999
bias_one = 0.99997344
bias_two = 0.095207853
adam_eps = 1e-08
norm_eps = 1e-06

f32 = jnp.float32
bf16 = jnp.bfloat16
MIB = 1 << 20
PARTS = ("row", "rep")
VM = pl.BlockSpec(memory_space=pltpu.VMEM)

A = ((1.0 - beta_two) / beta_two) ** 0.5
K = (1.0 - beta_one) / beta_one / A
C = beta_one / bias_one / (beta_two / bias_two) ** 0.5
E = adam_eps * bias_one / beta_one


def params(mib):
    return pltpu.CompilerParams(vmem_limit_bytes=mib * MIB)


def cost(flops, read):
    return pl.CostEstimate(flops=flops, bytes_accessed=read, transcendentals=0)


def swap(x, axis, n, k):
    return lax.ppermute(x, axis, [(a, a ^ k) for a in range(n)])


def place(parts, axis_sizes):
    index = 0
    for name, size in zip(parts, axis_sizes):
        index = index * size + lax.axis_index(name)
    return index


def encode_kernel(me_ref, *refs):
    rows, (bias_ref, w_ref), (rows_ref, *outs) = refs[:4], refs[4:6], refs[6:]
    x = jnp.concatenate([r[...] for r in rows], axis=0)
    rows_ref[...] = x
    centered = (x - bias_ref[...]).astype(bf16)
    chunk = outs[0].shape[1]
    wide = 512
    for k, out in enumerate(outs):
        start = jnp.bitwise_xor(me_ref[0], k) * chunk

        @pl.loop(0, chunk // wide)
        def _(t):
            s = pl.ds(pl.multiple_of(start + t * wide, 128), wide)
            out[:, pl.ds(pl.multiple_of(t * wide, 128), wide)] = jnp.dot(
                centered, w_ref[:, s], preferred_element_type=f32
            ).astype(bf16)


def encode(me, rows, bias, w, parts):
    depth, width = w.shape
    total = sum(r.shape[0] for r in rows)
    out = jax.ShapeDtypeStruct((total, width // parts), bf16)
    return pl.pallas_call(
        encode_kernel,
        in_specs=[pl.BlockSpec(memory_space=pltpu.SMEM)] + [VM] * (len(rows) + 2),
        out_specs=[VM] * (parts + 1),
        out_shape=[jax.ShapeDtypeStruct((total, depth), f32)] + [out] * parts,
        compiler_params=params(6),
        cost_estimate=cost(2 * total * depth * width, 2 * depth * width),
        name="encode",
    )(me, *rows, bias, pltpu.with_memory_space_constraint(w, pltpu.VMEM))


def active_kernel(me_ref, bias_ref, *refs):
    out = refs[-1]
    chunk = out.shape[1]
    total = refs[0][...].astype(f32)
    for r in refs[1:-1]:
        total = total + r[...].astype(f32)
    start = pl.multiple_of(me_ref[0] * chunk, 128)
    out[...] = jnp.maximum(total + bias_ref[:, pl.ds(start, chunk)], 0.0).astype(bf16)


def activate(me, bias, partials):
    return pl.pallas_call(
        active_kernel,
        in_specs=[pl.BlockSpec(memory_space=pltpu.SMEM)] + [VM] * (len(partials) + 1),
        out_specs=VM,
        out_shape=jax.ShapeDtypeStruct(partials[0].shape, bf16),
        compiler_params=params(4),
        name="activate",
    )(me, bias, *partials)


def squares_kernel(w_ref, out_ref):
    tall = 256
    one = jnp.ones((8, w_ref.shape[1]), bf16)

    @pl.loop(0, w_ref.shape[0] // tall)
    def _(t):
        w = w_ref[pl.ds(pl.multiple_of(t * tall, tall), tall), :]
        total = lax.dot_general(one, w * w, (((1,), (1,)), ((), ())), preferred_element_type=f32)
        out_ref[:, pl.ds(pl.multiple_of(t * tall, tall), tall)] = total[:1]


def squares(w):
    return pl.pallas_call(
        squares_kernel,
        in_specs=[VM],
        out_specs=VM,
        out_shape=jax.ShapeDtypeStruct((1, w.shape[0]), f32),
        compiler_params=params(4),
        cost_estimate=cost(16 * w.size, 2 * w.size),
        name="squares",
    )(w)


def rebuild_kernel(me_ref, *refs):
    parts = len(refs) - 3
    acts, w_ref, out_ref, all_ref = refs[:parts], refs[parts], refs[-2], refs[-1]
    chunk = acts[0].shape[1]
    tall = 1024
    total = jnp.zeros(out_ref.shape, f32)
    for k, act in enumerate(acts):
        start = jnp.bitwise_xor(me_ref[0], k) * chunk
        all_ref[:, pl.ds(pl.multiple_of(start, 128), chunk)] = act[...]

        def body(t, acc):
            rows = pl.ds(pl.multiple_of(start + t * tall, 128), tall)
            mine = act[:, pl.ds(pl.multiple_of(t * tall, 128), tall)]
            return acc + jnp.dot(mine, w_ref[rows, :], preferred_element_type=f32)

        total = lax.fori_loop(0, chunk // tall, body, total)
    out_ref[...] = total


def rebuild(me, acts, w):
    total = acts[0].shape[0]
    return pl.pallas_call(
        rebuild_kernel,
        in_specs=[pl.BlockSpec(memory_space=pltpu.SMEM)] + [VM] * (len(acts) + 1),
        out_specs=[VM, VM],
        out_shape=[
            jax.ShapeDtypeStruct((total, w.shape[1]), f32),
            jax.ShapeDtypeStruct((total, w.shape[0]), bf16),
        ],
        compiler_params=params(6),
        cost_estimate=cost(2 * total * w.size, 2 * w.size),
        name="rebuild",
    )(me, *acts, w)


def pair_kernel(mine_ref, other_ref, wide_ref, out_ref):
    groups = mine_ref.shape[0] // 8
    for q in range(groups):
        s = slice(8 * q, 8 * q + 8)
        wide_ref[s, :] = mine_ref[s, :] + pltpu.roll(other_ref[s, :], 4, 0)
    out_ref[...] = wide_ref[...].astype(bf16)


def pair_sum(mine, other):
    return pl.pallas_call(
        pair_kernel,
        in_specs=[VM, VM],
        out_specs=[VM, VM],
        out_shape=[
            jax.ShapeDtypeStruct(mine.shape, f32),
            jax.ShapeDtypeStruct(mine.shape, bf16),
        ],
        compiler_params=params(4),
        name="pair_sum",
    )(mine, other)


def adam_kernel(tall, block, acts_ref, mine_ref, o1, o2, o3, bias_ref, act_ref, s0, s1, s2, s3,
                w_ref, m_ref, v_ref, recon_ref, out_ref, right_ref, scale_ref):
    step = pl.program_id(0)
    total_rows, depth = mine_ref.shape
    local = recon_ref.shape[0]

    @pl.when(step == 0)
    def _():
        others = [o[...].astype(f32) for o in (o1, o2, o3)]
        pieces = []
        for q in range(total_rows // 8):
            piece = mine_ref[8 * q:8 * q + 8, :]
            for k, other in enumerate(others):
                p = q ^ (k + 1)
                piece = piece + other[8 * p:8 * p + 8]
            pieces.append(piece + bias_ref[...])
        rebuilt = jnp.concatenate(pieces, axis=0)
        recon_ref[...] = rebuilt[:local].astype(bf16)
        residual = (rebuilt - acts_ref[...]).astype(bf16)
        scaled = residual.astype(f32) * (A * 2.0 / total_rows)
        high = scaled.astype(bf16)
        low = (scaled - high.astype(f32)).astype(bf16)
        right_ref[...] = jnp.concatenate([high, low], axis=0)
        norm = lax.rsqrt((s0[...] + s1[...]) + (s2[...] + s3[...]) + norm_eps)
        counts = jnp.sum(act_ref[...].astype(f32), axis=0, keepdims=True)
        scale_ref[...] = (A * sparsity_coef / total_rows) * counts * norm

    right = right_ref[...]
    eye = (
        lax.broadcasted_iota(jnp.int32, (block, block), 0)
        == lax.broadcasted_iota(jnp.int32, (block, block), 1)
    )

    @pl.loop(0, tall // block)
    def _(b):
        here = pl.ds(pl.multiple_of(b * block, block), block)
        there = pl.ds(pl.multiple_of(step * tall + b * block, block), block)
        diag = jnp.where(eye, scale_ref[:, there], 0.0).astype(bf16)
        mine = act_ref[:, there].T
        left = jnp.concatenate([diag, mine, mine], axis=1)
        for c in range(0, depth, 256):
            cols = slice(c, min(c + 256, depth))
            both = jnp.concatenate([w_ref[there, cols], right[:, cols]], axis=0)
            g = jnp.dot(left, both, preferred_element_type=f32)
            x = v_ref[here, cols].astype(f32) + g * g
            r = lax.rsqrt(x)
            top = (m_ref[here, cols].astype(f32) + K * g) * r
            out_ref[here, cols] = (top * pltpu.reciprocal(E * r + 1.0 / C, approx=True)).astype(bf16)


def adam(acts, mine, others, bias, act, sums, w, m, v, local, tall=512, block=128):
    width, depth = w.shape
    total = mine.shape[0]
    tile = pl.BlockSpec((tall, depth), lambda i: (i, 0))
    return pl.pallas_call(
        functools.partial(adam_kernel, tall, block),
        grid=(width // tall,),
        in_specs=[VM] * 12 + [tile, tile],
        out_specs=[VM, tile],
        out_shape=[
            jax.ShapeDtypeStruct((local, depth), bf16),
            jax.ShapeDtypeStruct((width, depth), bf16),
        ],
        scratch_shapes=[pltpu.VMEM((2 * total, depth), bf16), pltpu.VMEM((1, width), f32)],
        compiler_params=params(16),
        cost_estimate=cost(8 * total * w.size, 6 * w.size),
        name="adam",
    )(
        acts, mine, *others, bias, act, *sums, w,
        pltpu.with_memory_space_constraint(m, pltpu.HBM),
        pltpu.with_memory_space_constraint(v, pltpu.HBM),
    )


def fast(sizes, activations, enc_weight, enc_bias, dec_weight, dec_bias, first_moment, second_moment):
    feat = sizes[0]
    parts = sizes[1] * sizes[2]
    local = activations.shape[0]
    me = place(PARTS, sizes[1:]).astype(jnp.int32).reshape(1)
    bias = dec_bias.reshape(1, -1)

    mine = activations.astype(f32)
    pair = jnp.concatenate([mine, swap(mine, "feat", feat, 1)], axis=0)
    rows = [pair] + [swap(pair, "feat", feat, k) for k in (2, 4, 6)]
    all_rows, *partials = encode(me, rows, bias, enc_weight, parts)
    partials = [partials[0]] + [swap(partials[k], PARTS, parts, k) for k in range(1, parts)]
    act = activate(me, enc_bias.reshape(1, -1), partials)
    acts = [act] + [swap(act, PARTS, parts, k) for k in range(1, parts)]

    w = pltpu.with_memory_space_constraint(dec_weight, pltpu.VMEM)
    sums = squares(w)
    sums = [sums] + [swap(sums, PARTS, parts, k) for k in range(1, parts)]
    part, all_act = rebuild(me, acts, w)
    part, narrow = pair_sum(part, swap(part, "feat", feat, 1))
    others = [swap(narrow, "feat", feat, k) for k in (2, 4, 6)]
    return adam(all_rows, part, others, bias, all_act, sums, w, first_moment, second_moment, local)


def plain(activations, enc_weight, enc_bias, dec_weight, dec_bias, first_moment, second_moment):
    local_rows = activations.shape[0]
    total_rows = local_rows * lax.axis_size("feat")
    centered = (activations.astype(f32) - dec_bias).astype(bf16)
    partial_value = jnp.dot(
        lax.all_gather(centered, "feat", axis=0, tiled=True), enc_weight, preferred_element_type=f32
    )
    wide = dec_weight.astype(f32)
    squares_sum = jnp.sum(wide * wide, axis=1)
    pre_sum, sum_squares = lax.psum((partial_value, squares_sum), PARTS)
    active = jnp.maximum(pre_sum + enc_bias, 0.0).astype(bf16)
    part = jnp.dot(active, dec_weight, preferred_element_type=f32)
    rebuilt = lax.psum_scatter(part, "feat", scatter_dimension=0, tiled=True) + dec_bias
    residual = (rebuilt - activations.astype(f32)).astype(bf16)
    all_residual = lax.all_gather(residual, "feat", axis=0, tiled=True)
    product = lax.dot_general(
        active, all_residual, (((0,), (0,)), ((), ())), preferred_element_type=f32
    )
    counts = jnp.sum(active.astype(f32), axis=0)
    row_norm = jnp.sqrt(sum_squares + norm_eps)
    gradient = (
        2.0 / total_rows * product
        + sparsity_coef / total_rows * counts[:, None] * wide / row_norm[:, None]
    )
    moment_one = beta_one * first_moment.astype(f32) + (1.0 - beta_one) * gradient
    moment_two = beta_two * second_moment.astype(f32) + (1.0 - beta_two) * gradient * gradient
    dec_step = moment_one / bias_one / (jnp.sqrt(moment_two / bias_two) + adam_eps)
    return rebuilt.astype(bf16), dec_step.astype(bf16)


def solution(mesh):
    sizes = tuple(mesh.shape[name] for name in ("feat", "row", "rep"))

    def shards(*args):
        local, depth = args[0].shape
        width = args[1].shape[1]
        fits = sizes[0] == 8 and local == 4 and depth % 128 == 0
        if fits and width % (1024 * sizes[1] * sizes[2]) == 0 and sizes[1] * sizes[2] == 4:
            return fast(sizes, *args)
        return plain(*args)

    split = P("feat", PARTS)
    return jax.shard_map(
        shards,
        mesh=mesh,
        in_specs=(split, P(PARTS, "feat"), P("feat"), split, P(PARTS), split, split),
        out_specs=(split, split),
        check_vma=False,
    )
```

time: 217 us -> 106 us (0.49)
  matrix products: 61 us -> 0 us
  waiting for transfers between devices: 74.6 us -> 20 us
  Pallas kernels: 0 us -> 54.4 us
  blocking collectives: 47.6 us -> 0 us
  starting transfers between devices: 0.08 us -> 21.7 us
  other arithmetic: 17.5 us -> 0.72 us
  between operations: 14.8 us -> 0.69 us
  local copies, waits for them, and re-layouts: 0.66 us -> 7.83 us
    dot_general x3 -> x0, matrix products: 61 us -> none  [the longest x1 41.7 us: shards(): lax.dot_general(active, all_residual, (((0,), (0,)), ((), ())), preferred...]
    pallas_call x0 -> x6, Pallas kernels: none -> 54.4 us  [the longest x1 35.8 us: adam(): pl.pallas_call(functools.partial(adam_kernel, tall, block), grid=(width /...]
    unnamed x3 -> x0, waiting for transfers between devices: 52.3 us -> none
    all_gather x2 -> x0, blocking collectives: 31.2 us -> none  [the longest x1 15.7 us: shards(): lax.all_gather(centered, 'feat', axis=0, tiled=True)]
    psum x1 -> x0, waiting for transfers between devices: 22.3 us -> none  [shards(): pre_sum, sum_squares = lax.psum((partial_value, squares), ('row', 'rep'))]
    ppermute x0 -> x17, starting transfers between devices: none -> 21.7 us  [swap(): return lax.ppermute(x, axis, [(a, a ^ k) for a in range(n)])]
    ppermute x0 -> x17, waiting for transfers between devices: none -> 20 us  [swap(): return lax.ppermute(x, axis, [(a, a ^ k) for a in range(n)])]
    psum x1 -> x0, blocking collectives: 16.4 us -> none  [shards(): pre_sum, sum_squares = lax.psum((partial_value, squares), ('row', 'rep'))]
  transfers between devices with their start and end apart: 2 -> 17, of which waited for: 2 -> 10; matrix products, arithmetic and copies ran while one was open for 7% -> 1% of each run, Pallas kernels for 0% -> 9%
where the time goes in v1:
time: 106 us; the launch traced here: 105 us
  Pallas kernels  54.4 us (51%)
  starting transfers between devices  21.7 us (20%)
  waiting for transfers between devices  20 us (19%)
  local copies, waits for them, and re-layouts  7.83 us (7%)
    pallas_call x1, Pallas kernels, adam(): pl.pallas_call(functools.partial(adam_kernel, tall, block), grid=(width /...  35.8 us
    ppermute x17, starting transfers between devices, swap(): return lax.ppermute(x, axis, [(a, a ^ k) for a in range(n)])  21.7 us
    ppermute x17, waiting for transfers between devices, swap(): return lax.ppermute(x, axis, [(a, a ^ k) for a in range(n)])  20 us
    pallas_call x1, Pallas kernels, squares(): pl.pallas_call(squares_kernel, in_specs=[VM], out_specs=VM, out_shape=jax...  9.25 us
    unnamed x6, local copies, waits for them, and re-layouts  7.13 us
    pallas_call x1, Pallas kernels, encode(): pl.pallas_call(encode_kernel, in_specs=[pl.BlockSpec(memory_space=pltpu.S...  5.11 us
    pallas_call x1, Pallas kernels, rebuild(): pl.pallas_call(rebuild_kernel, in_specs=[pl.BlockSpec(memory_space=pltpu....  4.19 us
  transfers between devices with their start and end apart: 17, of which 10 were waited for; matrix products, arithmetic and copies ran while one was open for 1% of the time, Pallas kernels for 9%

profile of v1, /device:TPU:0, one launch (start us, length us, event | category | flops | bytes accessed | tf_op | source)
XLA Modules:
  0.0 105.4 jit_solution(16499939736458406798)
XLA Ops:
  2.7 5.0 %collective-permute-start.3 = (f32[8,1152]{1,0:T(8,128)S(1)}, f32[8,1152]{1,0:T(8,128)S(1)}, u32[]{:S(2)}, u32[]{:S(2)}) collective-permute-start(f32[8,1152]{1,0:T(8,128)S(1)} %pad_maximum_fusion.refs_0_), channel_id=1, source_target_pairs={{0,24},{4,28},{8,16},{12,20},{16,8},{20,12},{24,0},{28,4},{1,25},{... | collective-permute-start | bytes 110600 | tf_op jit(solution)/shard_map/ppermute | solution.py:39
  9.6 2.9 %collective-permute-done.2.refs_2_ = f32[8,1152]{1,0:T(8,128)S(1)} collective-permute-done((f32[8,1152]{1,0:T(8,128)S(1)}, f32[8,1152]{1,0:T(8,128)S(1)}, u32[]{:S(2)}, u32[]{:S(2)}) %collective-permute-start.2) | collective-permute-done | bytes 36896 | tf_op jit(solution)/shard_map/ppermute | solution.py:39
  12.5 7.1 %copy-done.1 = bf16[1152,8192]{1,0:T(8,128)(2,1)S(1)} copy-done((bf16[1152,8192]{1,0:T(8,128)(2,1)S(1)}, bf16[1152,8192]{1,0:T(8,128)(2,1)}, u32[]{:S(2)}) %copy-start.1) | copy-done | bytes 18874392
  19.7 5.1 %encode.1 = (f32[32,1152]{1,0:T(8,128)S(1)}, bf16[32,2048]{1,0:T(8,128)(2,1)S(1)}, bf16[32,2048]{1,0:T(8,128)(2,1)S(1)}, bf16[32,2048]{1,0:T(8,128)(2,1)S(1)}, bf16[32,2048]{1,0:T(8,128)(2,1)S(1)}) custom-call(s32[1]{0:T(128)} %bitcast.me_ref, f32[8,1152]{1,0:T(8,128)S(1)} %pad_maximum_fusion.refs_0_, f32[8,1152]{1,0:T(8,128)S(1)} %collective-permute-done.1.refs_1_, ...), custom_call_target="tpu_custom_call" | custom-call | flops 603979776 | bytes 18874368 | tf_op jit(solution)/shard_map/encode/pallas_call | solution.py:71
  24.8 1.5 %collective-permute-start.4 = (bf16[32,2048]{1,0:T(8,128)(2,1)S(1)}, bf16[32,2048]{1,0:T(8,128)(2,1)S(1)}, u32[]{:S(2)}, u32[]{:S(2)}) collective-permute-start(bf16[32,2048]{1,0:T(8,128)(2,1)S(1)} %get-tuple-element.13), channel_id=1, source_target_pairs={{0,1},{1,0},{2,3},{3,2},{4,5},{5,4},{6,7},{7,6},{8,9},{9,8},{10,11... | collective-permute-start | bytes 393224 | tf_op jit(solution)/shard_map/ppermute | solution.py:39
  26.3 1.5 %collective-permute-start.5 = (bf16[32,2048]{1,0:T(8,128)(2,1)S(1)}, bf16[32,2048]{1,0:T(8,128)(2,1)S(1)}, u32[]{:S(2)}, u32[]{:S(2)}) collective-permute-start(bf16[32,2048]{1,0:T(8,128)(2,1)S(1)} %get-tuple-element.14), channel_id=1, source_target_pairs={{0,2},{1,3},{2,0},{3,1},{4,6},{5,7},{6,4},{7,5},{8,10},{9,11},{10,... | collective-permute-start | bytes 393224 | tf_op jit(solution)/shard_map/ppermute | solution.py:39
  28.3 2.4 %collective-permute-done.4.refs_1_ = bf16[32,2048]{1,0:T(8,128)(2,1)S(1)} collective-permute-done((bf16[32,2048]{1,0:T(8,128)(2,1)S(1)}, bf16[32,2048]{1,0:T(8,128)(2,1)S(1)}, u32[]{:S(2)}, u32[]{:S(2)}) %collective-permute-start.4) | collective-permute-done | bytes 131104 | tf_op jit(solution)/shard_map/ppermute | solution.py:39
  30.7 3.4 %collective-permute-done.5.refs_2_ = bf16[32,2048]{1,0:T(8,128)(2,1)S(1)} collective-permute-done((bf16[32,2048]{1,0:T(8,128)(2,1)S(1)}, bf16[32,2048]{1,0:T(8,128)(2,1)S(1)}, u32[]{:S(2)}, u32[]{:S(2)}) %collective-permute-start.5) | collective-permute-done | bytes 131104 | tf_op jit(solution)/shard_map/ppermute | solution.py:39
  34.1 0.9 collective-permute-start.9
  35.1 1.2 %collective-permute-start.8 = (bf16[32,2048]{1,0:T(8,128)(2,1)S(1)}, bf16[32,2048]{1,0:T(8,128)(2,1)S(1)}, u32[]{:S(2)}, u32[]{:S(2)}) collective-permute-start(bf16[32,2048]{1,0:T(8,128)(2,1)S(1)} %activate.1.refs_0_), channel_id=1, source_target_pairs={{0,2},{1,3},{2,0},{3,1},{4,6},{5,7},{6,4},{7,5},{8,10},{9,11},{10,... | collective-permute-start | bytes 393224 | tf_op jit(solution)/shard_map/ppermute | solution.py:39
  36.2 1.5 %collective-permute-start.7 = (bf16[32,2048]{1,0:T(8,128)(2,1)S(1)}, bf16[32,2048]{1,0:T(8,128)(2,1)S(1)}, u32[]{:S(2)}, u32[]{:S(2)}) collective-permute-start(bf16[32,2048]{1,0:T(8,128)(2,1)S(1)} %activate.1.refs_0_), channel_id=1, source_target_pairs={{0,1},{1,0},{2,3},{3,2},{4,5},{5,4},{6,7},{7,6},{8,9},{9,8},{10,11... | collective-permute-start | bytes 393224 | tf_op jit(solution)/shard_map/ppermute | solution.py:39
  37.7 2.5 %collective-permute-done.9.refs_3_ = bf16[32,2048]{1,0:T(8,128)(2,1)S(1)} collective-permute-done((bf16[32,2048]{1,0:T(8,128)(2,1)S(1)}, bf16[32,2048]{1,0:T(8,128)(2,1)S(1)}, u32[]{:S(2)}, u32[]{:S(2)}) %collective-permute-start.9) | collective-permute-done | bytes 131104 | tf_op jit(solution)/shard_map/ppermute | solution.py:39
  40.2 1.2 %collective-permute-done.8.refs_2_ = bf16[32,2048]{1,0:T(8,128)(2,1)S(1)} collective-permute-done((bf16[32,2048]{1,0:T(8,128)(2,1)S(1)}, bf16[32,2048]{1,0:T(8,128)(2,1)S(1)}, u32[]{:S(2)}, u32[]{:S(2)}) %collective-permute-start.8) | collective-permute-done | bytes 131104 | tf_op jit(solution)/shard_map/ppermute | solution.py:39
  41.4 4.2 %rebuild.1 = (f32[32,1152]{1,0:T(8,128)S(1)}, bf16[32,8192]{1,0:T(8,128)(2,1)S(1)}) custom-call(s32[1]{0:T(128)} %bitcast.me_ref, bf16[32,2048]{1,0:T(8,128)(2,1)S(1)} %activate.1.refs_0_, bf16[32,2048]{1,0:T(8,128)(2,1)S(1)} %collective-permute-done.7.refs_1_, bf16[32,2048]{1,0:T(8,128)(2,1)S(1)} %collective-permute-done.8.refs_2_, ...), custom_call_target="tpu_custom_call" | custom-call | flops 603979776 | bytes 18874368 | tf_op jit(solution)/shard_map/rebuild/pallas_call | solution.py:147
  45.7 1.4 %collective-permute-done.10.other_ref = f32[32,1152]{1,0:T(8,128)S(1)} collective-permute-done((f32[32,1152]{1,0:T(8,128)S(1)}, f32[32,1152]{1,0:T(8,128)S(1)}, u32[]{:S(2)}, u32[]{:S(2)}) %collective-permute-start.10) | collective-permute-done | bytes 147488 | tf_op jit(solution)/shard_map/ppermute | solution.py:39
  47.1 1.3 %collective-permute-start.13 = (bf16[32,1152]{1,0:T(8,128)(2,1)S(1)}, bf16[32,1152]{1,0:T(8,128)(2,1)S(1)}, u32[]{:S(2)}, u32[]{:S(2)}) collective-permute-start(bf16[32,1152]{1,0:T(8,128)(2,1)S(1)} %get-tuple-element.18), channel_id=1, source_target_pairs={{0,24},{4,28},{8,16},{12,20},{16,8},{20,12},{24,0},{28,4},{1,25},{... | collective-permute-start | bytes 221192 | tf_op jit(solution)/shard_map/ppermute | solution.py:39
  48.9 2.6 %collective-permute-start.11 = (bf16[32,1152]{1,0:T(8,128)(2,1)S(1)}, bf16[32,1152]{1,0:T(8,128)(2,1)S(1)}, u32[]{:S(2)}, u32[]{:S(2)}) collective-permute-start(bf16[32,1152]{1,0:T(8,128)(2,1)S(1)} %get-tuple-element.18), channel_id=1, source_target_pairs={{0,8},{4,12},{8,0},{12,4},{16,24},{20,28},{24,16},{28,20},{1,9},{5... | collective-permute-start | bytes 221192 | tf_op jit(solution)/shard_map/ppermute | solution.py:39
  51.6 9.3 %squares.1.s0 = f32[1,8192]{1,0:T(1,128)S(1)} custom-call(bf16[8192,1152]{1,0:T(8,128)(2,1)S(1)} %copy-done), custom_call_target="tpu_custom_call" | custom-call | flops 150994944 | bytes 18874368 | tf_op jit(solution)/shard_map/squares/pallas_call | solution.py:115
  60.8 1.7 %collective-permute-start.16 = (f32[1,8192]{1,0:T(1,128)S(1)}, f32[1,8192]{1,0:T(1,128)S(1)}, u32[]{:S(2)}, u32[]{:S(2)}) collective-permute-start(f32[1,8192]{1,0:T(1,128)S(1)} %squares.1.s0), channel_id=1, source_target_pairs={{0,3},{1,2},{2,1},{3,0},{4,7},{5,6},{6,5},{7,4},{8,11},{9,10},{10,... | collective-permute-start | bytes 98312 | tf_op jit(solution)/shard_map/ppermute | solution.py:39
  62.5 1.0 collective-permute-start.15
  63.6 2.1 %collective-permute-done.16.s3 = f32[1,8192]{1,0:T(1,128)S(1)} collective-permute-done((f32[1,8192]{1,0:T(1,128)S(1)}, f32[1,8192]{1,0:T(1,128)S(1)}, u32[]{:S(2)}, u32[]{:S(2)}) %collective-permute-start.16) | collective-permute-done | bytes 32800 | tf_op jit(solution)/shard_map/ppermute | solution.py:39
  65.7 1.2 %collective-permute-start.14 = (f32[1,8192]{1,0:T(1,128)S(1)}, f32[1,8192]{1,0:T(1,128)S(1)}, u32[]{:S(2)}, u32[]{:S(2)}) collective-permute-start(f32[1,8192]{1,0:T(1,128)S(1)} %squares.1.s0), channel_id=1, source_target_pairs={{0,1},{1,0},{2,3},{3,2},{4,5},{5,4},{6,7},{7,6},{8,9},{9,8},{10,11... | collective-permute-start | bytes 98312 | tf_op jit(solution)/shard_map/ppermute | solution.py:39
  66.9 2.7 %collective-permute-done.14.s1 = f32[1,8192]{1,0:T(1,128)S(1)} collective-permute-done((f32[1,8192]{1,0:T(1,128)S(1)}, f32[1,8192]{1,0:T(1,128)S(1)}, u32[]{:S(2)}, u32[]{:S(2)}) %collective-permute-start.14) | collective-permute-done | bytes 32800 | tf_op jit(solution)/shard_map/ppermute | solution.py:39
  69.6 35.8 %adam.1 = (bf16[4,1152]{1,0:T(4,128)(2,1)}, bf16[8192,1152]{1,0:T(8,128)(2,1)}) custom-call(f32[32,1152]{1,0:T(8,128)S(1)} %get-tuple-element.11.acts_ref, f32[32,1152]{1,0:T(8,128)S(1)} %get-tuple-element.17.mine_ref, bf16[32,1152]{1,0:T(8,128)(2,1)S(1)} %collective-permute-done.11.o1, bf16[32,1152]{1,0:T(8,128)(2,1)S(1)} %collective-permute-done.12.o2, ...), custom_call_target="tpu_custom_call" | custom-call | flops 2415919104 | bytes 56623104 | tf_op jit(solution)/shard_map/adam/pallas_call | solution.py:237
  (25 shorter events, 5.2 us)
Async XLA Ops:
  0.6 33.4 %copy-start.2 = (f32[8192]{0:T(1024)S(1)}, f32[8192]{0:T(1024)}, u32[]{:S(2)}) copy-start(f32[8192]{0:T(1024)} %param.9) | copy-start | bytes 98308
  1.3 1.3 %collective-permute-start = (f32[4,1152]{1,0:T(4,128)S(1)}, f32[4,1152]{1,0:T(4,128)S(1)}, u32[]{:S(2)}, u32[]{:S(2)}) collective-permute-start(f32[4,1152]{1,0:T(4,128)S(1)} %convert_element_type.3), channel_id=1, source_target_pairs={{0,4},{4,0},{8,12},{12,8},{16,20},{20,16},{24,28},{28,24},{1,5},{5... | collective-permute-start | bytes 55304 | tf_op jit(solution)/shard_map/ppermute | solution.py:39
  2.7 7.0 %collective-permute-start.3 = (f32[8,1152]{1,0:T(8,128)S(1)}, f32[8,1152]{1,0:T(8,128)S(1)}, u32[]{:S(2)}, u32[]{:S(2)}) collective-permute-start(f32[8,1152]{1,0:T(8,128)S(1)} %pad_maximum_fusion.refs_0_), channel_id=1, source_target_pairs={{0,24},{4,28},{8,16},{12,20},{16,8},{20,12},{24,0},{28,4},{1,25},{... | collective-permute-start | bytes 110600 | tf_op jit(solution)/shard_map/ppermute | solution.py:39
  7.7 4.9 %collective-permute-start.2 = (f32[8,1152]{1,0:T(8,128)S(1)}, f32[8,1152]{1,0:T(8,128)S(1)}, u32[]{:S(2)}, u32[]{:S(2)}) collective-permute-start(f32[8,1152]{1,0:T(8,128)S(1)} %pad_maximum_fusion.refs_0_), channel_id=1, source_target_pairs={{0,16},{4,20},{8,24},{12,28},{16,0},{20,4},{24,8},{28,12},{1,17},{... | collective-permute-start | bytes 110600 | tf_op jit(solution)/shard_map/ppermute | solution.py:39
  7.7 4.9 %collective-permute-start.1 = (f32[8,1152]{1,0:T(8,128)S(1)}, f32[8,1152]{1,0:T(8,128)S(1)}, u32[]{:S(2)}, u32[]{:S(2)}) collective-permute-start(f32[8,1152]{1,0:T(8,128)S(1)} %pad_maximum_fusion.refs_0_), channel_id=1, source_target_pairs={{0,8},{4,12},{8,0},{12,4},{16,24},{20,28},{24,16},{28,20},{1,9},{5... | collective-permute-start | bytes 110600 | tf_op jit(solution)/shard_map/ppermute | solution.py:39
  9.0 32.4 %copy-start = (bf16[8192,1152]{1,0:T(8,128)(2,1)S(1)}, bf16[8192,1152]{1,0:T(8,128)(2,1)}, u32[]{:S(2)}) copy-start(bf16[8192,1152]{1,0:T(8,128)(2,1)} %w_ref.3) | copy-start | bytes 56623108
  12.5 7.1 %copy-start.1 = (bf16[1152,8192]{1,0:T(8,128)(2,1)S(1)}, bf16[1152,8192]{1,0:T(8,128)(2,1)}, u32[]{:S(2)}) copy-start(bf16[1152,8192]{1,0:T(8,128)(2,1)} %refs_5_.1) | copy-start | bytes 56623108
  24.8 5.9 %collective-permute-start.4 = (bf16[32,2048]{1,0:T(8,128)(2,1)S(1)}, bf16[32,2048]{1,0:T(8,128)(2,1)S(1)}, u32[]{:S(2)}, u32[]{:S(2)}) collective-permute-start(bf16[32,2048]{1,0:T(8,128)(2,1)S(1)} %get-tuple-element.13), channel_id=1, source_target_pairs={{0,1},{1,0},{2,3},{3,2},{4,5},{5,4},{6,7},{7,6},{8,9},{9,8},{10,11... | collective-permute-start | bytes 393224 | tf_op jit(solution)/shard_map/ppermute | solution.py:39
  26.3 7.8 %collective-permute-start.5 = (bf16[32,2048]{1,0:T(8,128)(2,1)S(1)}, bf16[32,2048]{1,0:T(8,128)(2,1)S(1)}, u32[]{:S(2)}, u32[]{:S(2)}) collective-permute-start(bf16[32,2048]{1,0:T(8,128)(2,1)S(1)} %get-tuple-element.14), channel_id=1, source_target_pairs={{0,2},{1,3},{2,0},{3,1},{4,6},{5,7},{6,4},{7,5},{8,10},{9,11},{10,... | collective-permute-start | bytes 393224 | tf_op jit(solution)/shard_map/ppermute | solution.py:39
  27.8 6.3 %collective-permute-start.6 = (bf16[32,2048]{1,0:T(8,128)(2,1)S(1)}, bf16[32,2048]{1,0:T(8,128)(2,1)S(1)}, u32[]{:S(2)}, u32[]{:S(2)}) collective-permute-start(bf16[32,2048]{1,0:T(8,128)(2,1)S(1)} %get-tuple-element.15), channel_id=1, source_target_pairs={{0,3},{1,2},{2,1},{3,0},{4,7},{5,6},{6,5},{7,4},{8,11},{9,10},{10,... | collective-permute-start | bytes 393224 | tf_op jit(solution)/shard_map/ppermute | solution.py:39
  34.1 6.0 %collective-permute-start.9 = (bf16[32,2048]{1,0:T(8,128)(2,1)S(1)}, bf16[32,2048]{1,0:T(8,128)(2,1)S(1)}, u32[]{:S(2)}, u32[]{:S(2)}) collective-permute-start(bf16[32,2048]{1,0:T(8,128)(2,1)S(1)} %activate.1.refs_0_), channel_id=1, source_target_pairs={{0,3},{1,2},{2,1},{3,0},{4,7},{5,6},{6,5},{7,4},{8,11},{9,10},{10,... | collective-permute-start | bytes 393224 | tf_op jit(solution)/shard_map/ppermute | solution.py:39
  35.1 6.4 %collective-permute-start.8 = (bf16[32,2048]{1,0:T(8,128)(2,1)S(1)}, bf16[32,2048]{1,0:T(8,128)(2,1)S(1)}, u32[]{:S(2)}, u32[]{:S(2)}) collective-permute-start(bf16[32,2048]{1,0:T(8,128)(2,1)S(1)} %activate.1.refs_0_), channel_id=1, source_target_pairs={{0,2},{1,3},{2,0},{3,1},{4,6},{5,7},{6,4},{7,5},{8,10},{9,11},{10,... | collective-permute-start | bytes 393224 | tf_op jit(solution)/shard_map/ppermute | solution.py:39
  36.2 5.2 %collective-permute-start.7 = (bf16[32,2048]{1,0:T(8,128)(2,1)S(1)}, bf16[32,2048]{1,0:T(8,128)(2,1)S(1)}, u32[]{:S(2)}, u32[]{:S(2)}) collective-permute-start(bf16[32,2048]{1,0:T(8,128)(2,1)S(1)} %activate.1.refs_0_), channel_id=1, source_target_pairs={{0,1},{1,0},{2,3},{3,2},{4,5},{5,4},{6,7},{7,6},{8,9},{9,8},{10,11... | collective-permute-start | bytes 393224 | tf_op jit(solution)/shard_map/ppermute | solution.py:39
  45.6 1.4 %collective-permute-start.10 = (f32[32,1152]{1,0:T(8,128)S(1)}, f32[32,1152]{1,0:T(8,128)S(1)}, u32[]{:S(2)}, u32[]{:S(2)}) collective-permute-start(f32[32,1152]{1,0:T(8,128)S(1)} %get-tuple-element.16.mine_ref), channel_id=1, source_target_pairs={{0,4},{4,0},{8,12},{12,8},{16,20},{20,16},{24,28},{28,24},{1,5},{5... | collective-permute-start | bytes 442376 | tf_op jit(solution)/shard_map/ppermute | solution.py:39
  47.1 22.5 %collective-permute-start.13 = (bf16[32,1152]{1,0:T(8,128)(2,1)S(1)}, bf16[32,1152]{1,0:T(8,128)(2,1)S(1)}, u32[]{:S(2)}, u32[]{:S(2)}) collective-permute-start(bf16[32,1152]{1,0:T(8,128)(2,1)S(1)} %get-tuple-element.18), channel_id=1, source_target_pairs={{0,24},{4,28},{8,16},{12,20},{16,8},{20,12},{24,0},{28,4},{1,25},{... | collective-permute-start | bytes 221192 | tf_op jit(solution)/shard_map/ppermute | solution.py:39
  48.4 21.2 %collective-permute-start.12 = (bf16[32,1152]{1,0:T(8,128)(2,1)S(1)}, bf16[32,1152]{1,0:T(8,128)(2,1)S(1)}, u32[]{:S(2)}, u32[]{:S(2)}) collective-permute-start(bf16[32,1152]{1,0:T(8,128)(2,1)S(1)} %get-tuple-element.18), channel_id=1, source_target_pairs={{0,16},{4,20},{8,24},{12,28},{16,0},{20,4},{24,8},{28,12},{1,17},{... | collective-permute-start | bytes 221192 | tf_op jit(solution)/shard_map/ppermute | solution.py:39
  48.9 20.7 %collective-permute-start.11 = (bf16[32,1152]{1,0:T(8,128)(2,1)S(1)}, bf16[32,1152]{1,0:T(8,128)(2,1)S(1)}, u32[]{:S(2)}, u32[]{:S(2)}) collective-permute-start(bf16[32,1152]{1,0:T(8,128)(2,1)S(1)} %get-tuple-element.18), channel_id=1, source_target_pairs={{0,8},{4,12},{8,0},{12,4},{16,24},{20,28},{24,16},{28,20},{1,9},{5... | collective-permute-start | bytes 221192 | tf_op jit(solution)/shard_map/ppermute | solution.py:39
  60.8 4.9 %collective-permute-start.16 = (f32[1,8192]{1,0:T(1,128)S(1)}, f32[1,8192]{1,0:T(1,128)S(1)}, u32[]{:S(2)}, u32[]{:S(2)}) collective-permute-start(f32[1,8192]{1,0:T(1,128)S(1)} %squares.1.s0), channel_id=1, source_target_pairs={{0,3},{1,2},{2,1},{3,0},{4,7},{5,6},{6,5},{7,4},{8,11},{9,10},{10,... | collective-permute-start | bytes 98312 | tf_op jit(solution)/shard_map/ppermute | solution.py:39
  62.5 4.4 %collective-permute-start.15 = (f32[1,8192]{1,0:T(1,128)S(1)}, f32[1,8192]{1,0:T(1,128)S(1)}, u32[]{:S(2)}, u32[]{:S(2)}) collective-permute-start(f32[1,8192]{1,0:T(1,128)S(1)} %squares.1.s0), channel_id=1, source_target_pairs={{0,2},{1,3},{2,0},{3,1},{4,6},{5,7},{6,4},{7,5},{8,10},{9,11},{10,... | collective-permute-start | bytes 98312 | tf_op jit(solution)/shard_map/ppermute | solution.py:39
  65.7 3.9 %collective-permute-start.14 = (f32[1,8192]{1,0:T(1,128)S(1)}, f32[1,8192]{1,0:T(1,128)S(1)}, u32[]{:S(2)}, u32[]{:S(2)}) collective-permute-start(f32[1,8192]{1,0:T(1,128)S(1)} %squares.1.s0), channel_id=1, source_target_pairs={{0,1},{1,0},{2,3},{3,2},{4,5},{5,4},{6,7},{7,6},{8,9},{9,8},{10,11... | collective-permute-start | bytes 98312 | tf_op jit(solution)/shard_map/ppermute | solution.py:39

commit v2 on v1

v2 whole, which is shorter than its diff:
```python
import functools

import jax
import jax.experimental.pallas as pl
import jax.experimental.pallas.tpu as pltpu
import jax.numpy as jnp
from jax import lax
from jax.sharding import PartitionSpec as P

sparsity_coef = 5.0
beta_one = 0.9
beta_two = 0.999
bias_one = 0.99997344
bias_two = 0.095207853
adam_eps = 1e-08
norm_eps = 1e-06

f32 = jnp.float32
bf16 = jnp.bfloat16
MIB = 1 << 20
TALL = 1024
PARTS = ("row", "rep")
VM = pl.BlockSpec(memory_space=pltpu.VMEM)
HBM = pl.BlockSpec(memory_space=pltpu.HBM)
ANY = pl.BlockSpec(memory_space=pl.ANY)

A = ((1.0 - beta_two) / beta_two) ** 0.5
K = (1.0 - beta_one) / beta_one / A
C = beta_one / bias_one / (beta_two / bias_two) ** 0.5
E = adam_eps * bias_one / beta_one


def params(mib):
    return pltpu.CompilerParams(vmem_limit_bytes=mib * MIB)


def cost(flops, read):
    return pl.CostEstimate(flops=flops, bytes_accessed=read, transcendentals=0)


def swap(x, axis, n, k):
    return lax.ppermute(x, axis, [(a, a ^ k) for a in range(n)])


def place(parts, axis_sizes):
    index = 0
    for name, size in zip(parts, axis_sizes):
        index = index * size + lax.axis_index(name)
    return index


def widen_kernel(x_ref, bias_ref, out_ref, same_ref):
    out_ref[...] = x_ref[...].astype(f32)
    same_ref[...] = bias_ref[...]


def widen(x, bias):
    return pl.pallas_call(
        widen_kernel,
        in_specs=[VM, VM],
        out_specs=[VM, VM],
        out_shape=[jax.ShapeDtypeStruct(x.shape, f32), jax.ShapeDtypeStruct(bias.shape, f32)],
        compiler_params=params(4),
        name="widen",
    )(x, bias)


def join_kernel(mine_ref, other_ref, out_ref):
    out_ref[...] = jnp.concatenate([mine_ref[...], other_ref[...].astype(f32)], axis=0)


def join(mine, other):
    return pl.pallas_call(
        join_kernel,
        in_specs=[VM, VM],
        out_specs=VM,
        out_shape=jax.ShapeDtypeStruct((2 * mine.shape[0], mine.shape[1]), f32),
        compiler_params=params(4),
        name="join",
    )(mine, other)


def center_kernel(*refs):
    rows, (bias_ref, rows_ref, out_ref) = refs[:-3], refs[-3:]
    x = jnp.concatenate([r[...] for r in rows], axis=0)
    rows_ref[...] = x
    out_ref[...] = (x - bias_ref[...]).astype(bf16)


def center(rows, bias):
    shape = (sum(r.shape[0] for r in rows), bias.shape[1])
    return pl.pallas_call(
        center_kernel,
        in_specs=[VM] * (len(rows) + 1),
        out_specs=[VM, VM],
        out_shape=[jax.ShapeDtypeStruct(shape, f32), jax.ShapeDtypeStruct(shape, bf16)],
        compiler_params=params(4),
        name="center",
    )(*rows, bias)


def columns(me_ref, k, chunk):
    return pl.ds(pl.multiple_of(jnp.bitwise_xor(me_ref[0], k) * chunk, 128), chunk)


PIECES = 4


def strip_copies(me_ref, k, w_ref, out_ref, sems, first=0):
    depth, chunk = out_ref.shape
    rows = depth // PIECES
    return [
        pltpu.make_async_copy(
            w_ref.at[pl.ds(p * rows, rows), columns(me_ref, k, chunk)],
            out_ref.at[pl.ds(p * rows, rows)],
            sems.at[first + p],
        )
        for p in range(PIECES)
    ]


def fetch_kernel(ks, me_ref, w_ref, _, *refs):
    outs, sems = refs[:-1], refs[-1]
    copies = []
    for i, (k, out) in enumerate(zip(ks, outs)):
        copies += strip_copies(me_ref, k, w_ref, out, sems, i * PIECES)
    for copy in copies:
        copy.start()
    for copy in copies:
        copy.wait()


def fetch(ks, me, w, after, parts):
    depth, width = w.shape
    return pl.pallas_call(
        functools.partial(fetch_kernel, ks),
        in_specs=[pl.BlockSpec(memory_space=pltpu.SMEM), HBM, ANY],
        out_specs=[VM] * len(ks),
        out_shape=[pltpu.VMEM((depth, width // parts), bf16)] * len(ks),
        scratch_shapes=[pltpu.SemaphoreType.DMA((len(ks) * PIECES,))],
        compiler_params=params(4),
        cost_estimate=cost(0, 2 * len(ks) * depth * width // parts),
        name="fetch",
    )(me, pltpu.with_memory_space_constraint(w, pltpu.HBM), after)


def encode_kernel(ahead, me_ref, x_ref, here_ref, *refs):
    out_ref = refs[-1] if ahead is None else refs[1]
    chunk = out_ref.shape[1]
    wide = 512
    copies = []
    if ahead is not None:
        copies = strip_copies(me_ref, ahead, refs[0], refs[2], refs[3])
    for copy in copies:
        copy.start()

    @pl.loop(0, chunk // wide)
    def _(t):
        s = pl.ds(pl.multiple_of(t * wide, 128), wide)
        out_ref[:, s] = jnp.dot(
            x_ref[...], here_ref[:, s], preferred_element_type=f32
        ).astype(bf16)

    for copy in copies:
        copy.wait()


def encode(me, x, here, w=None, ahead=None):
    total, (depth, chunk) = x.shape[0], here.shape
    out = jax.ShapeDtypeStruct((total, chunk), bf16)
    more = ahead is not None
    return pl.pallas_call(
        functools.partial(encode_kernel, ahead),
        in_specs=[pl.BlockSpec(memory_space=pltpu.SMEM), VM, VM] + [HBM] * more,
        out_specs=[VM, VM] if more else VM,
        out_shape=[out, pltpu.VMEM((depth, chunk), bf16)] if more else out,
        scratch_shapes=[pltpu.SemaphoreType.DMA((PIECES,))] * more,
        compiler_params=params(4),
        cost_estimate=cost(2 * total * depth * chunk, 2 * depth * chunk),
        name="encode",
    )(me, x, here, *([pltpu.with_memory_space_constraint(w, pltpu.HBM)] if more else []))


def active_kernel(me_ref, bias_ref, *refs):
    out = refs[-1]
    chunk = out.shape[1]
    total = refs[0][...].astype(f32)
    for r in refs[1:-1]:
        total = total + r[...].astype(f32)
    start = pl.multiple_of(me_ref[0] * chunk, 128)
    out[...] = jnp.maximum(total + bias_ref[:, pl.ds(start, chunk)], 0.0).astype(bf16)


def activate(me, bias, partials):
    return pl.pallas_call(
        active_kernel,
        in_specs=[pl.BlockSpec(memory_space=pltpu.SMEM)] + [VM] * (len(partials) + 1),
        out_specs=VM,
        out_shape=jax.ShapeDtypeStruct(partials[0].shape, bf16),
        compiler_params=params(4),
        name="activate",
    )(me, bias, *partials)


def squares_kernel(w_ref, _, out_ref):
    tall = 256

    @pl.loop(0, w_ref.shape[0] // TALL)
    def _(i):
        for c in range(0, TALL, tall):
            rows = pl.ds(pl.multiple_of(i * TALL + c, tall), tall)
            total = jnp.zeros((tall, 128), f32)
            for d in range(0, w_ref.shape[1], 128):
                w = w_ref[rows, d:d + 128].astype(f32)
                total = total + w * w
            out_ref[pl.ds(i, 1), c:c + tall] = jnp.sum(total.T, axis=0, keepdims=True)


def squares(w, after):
    return pl.pallas_call(
        squares_kernel,
        in_specs=[VM, ANY],
        out_specs=VM,
        out_shape=jax.ShapeDtypeStruct((w.shape[0] // TALL, TALL), f32),
        compiler_params=params(4),
        cost_estimate=cost(2 * w.size, 2 * w.size),
        name="squares",
    )(w, after)


def rebuild_part(k, me_ref, act_ref, w_ref, total):
    chunk = act_ref.shape[1]
    tall = 1024
    start = jnp.bitwise_xor(me_ref[0], k) * chunk

    def body(t, acc):
        rows = pl.ds(pl.multiple_of(start + t * tall, 128), tall)
        mine = act_ref[:, pl.ds(pl.multiple_of(t * tall, 128), tall)]
        return acc + jnp.dot(mine, w_ref[rows, :], preferred_element_type=f32)

    return lax.fori_loop(0, chunk // tall, body, total)


def rebuild_own_kernel(me_ref, act_ref, w_ref, out_ref):
    out_ref[...] = rebuild_part(0, me_ref, act_ref, w_ref, jnp.zeros(out_ref.shape, f32))


def rebuild_kernel(me_ref, part_ref, *refs):
    acts, w_ref, (out_ref, all_ref, counts_ref) = refs[:-4], refs[-4], refs[-3:]
    chunk = acts[0].shape[1]
    total = part_ref[...]
    for k, act in enumerate(acts):
        here = columns(me_ref, k, chunk)
        all_ref[:, here] = act[...]
        for c in range(0, chunk, TALL):
            row = jnp.bitwise_xor(me_ref[0], k) * (chunk // TALL) + c // TALL
            counts_ref[pl.ds(row, 1), :] = jnp.sum(
                act[:, c:c + TALL].astype(f32), axis=0, keepdims=True
            )
        if k:
            total = rebuild_part(k, me_ref, act, w_ref, total)
    out_ref[...] = total


def rebuild_own(me, act, w):
    (total, chunk), depth = act.shape, w.shape[1]
    return pl.pallas_call(
        rebuild_own_kernel,
        in_specs=[pl.BlockSpec(memory_space=pltpu.SMEM), VM, VM],
        out_specs=VM,
        out_shape=jax.ShapeDtypeStruct((total, depth), f32),
        compiler_params=params(4),
        cost_estimate=cost(2 * total * chunk * depth, 2 * chunk * depth),
        name="rebuild_own",
    )(me, act, w)


def rebuild(me, part, acts, w):
    total, (width, depth) = acts[0].shape[0], w.shape
    return pl.pallas_call(
        rebuild_kernel,
        in_specs=[pl.BlockSpec(memory_space=pltpu.SMEM)] + [VM] * (len(acts) + 2),
        out_specs=[VM] * 3,
        out_shape=[
            jax.ShapeDtypeStruct((total, depth), f32),
            jax.ShapeDtypeStruct((total, width), bf16),
            jax.ShapeDtypeStruct((width // TALL, TALL), f32),
        ],
        compiler_params=params(4),
        cost_estimate=cost(2 * total * w.size, 2 * w.size),
        name="rebuild",
    )(me, part, *acts, w)


def add_kernel(a_ref, b_ref, out_ref):
    out_ref[...] = a_ref[...] + b_ref[...]


def add(a, b):
    return pl.pallas_call(
        add_kernel,
        in_specs=[VM, VM],
        out_specs=VM,
        out_shape=jax.ShapeDtypeStruct(a.shape, a.dtype),
        compiler_params=params(4),
        name="add",
    )(a, b)


def pair_kernel(mine_ref, other_ref, wide_ref, out_ref):
    groups = mine_ref.shape[0] // 8
    for q in range(groups):
        s = slice(8 * q, 8 * q + 8)
        wide_ref[s, :] = mine_ref[s, :] + pltpu.roll(other_ref[s, :], 4, 0)
    out_ref[...] = wide_ref[...].astype(bf16)


def pair_sum(mine, other):
    return pl.pallas_call(
        pair_kernel,
        in_specs=[VM, VM],
        out_specs=[VM, VM],
        out_shape=[
            jax.ShapeDtypeStruct(mine.shape, f32),
            jax.ShapeDtypeStruct(mine.shape, bf16),
        ],
        compiler_params=params(4),
        name="pair_sum",
    )(mine, other)


def adam_kernel(tall, block, acts_ref, mine_ref, o1, o2, o3, bias_ref, act_ref, counts_ref, s0, s1,
                w_ref, m_hbm, v_hbm, recon_ref, out_hbm, right_ref, scale_ref, m_buf, v_buf, out_buf,
                m_sems, v_sems, out_sems):
    total_rows, depth = mine_ref.shape
    local = recon_ref.shape[0]
    steps = w_ref.shape[0] // tall
    slots, out_slots = m_buf.shape[0], out_buf.shape[0]

    def tile(ref, i):
        return ref.at[pl.ds(pl.multiple_of(i * tall, tall), tall)]

    def loads(i):
        slot = lax.rem(i, slots)
        return (
            pltpu.make_async_copy(tile(m_hbm, i), m_buf.at[slot], m_sems.at[slot]),
            pltpu.make_async_copy(tile(v_hbm, i), v_buf.at[slot], v_sems.at[slot]),
        )

    def store(i):
        slot = lax.rem(i, out_slots)
        return pltpu.make_async_copy(out_buf.at[slot], tile(out_hbm, i), out_sems.at[slot])

    for i in range(slots):
        for copy in loads(i):
            copy.start()

    others = [o[...].astype(f32) for o in (o1, o2, o3)]
    pieces = []
    for q in range(total_rows // 8):
        piece = mine_ref[8 * q:8 * q + 8, :]
        for k, other in enumerate(others):
            p = q ^ (k + 1)
            piece = piece + other[8 * p:8 * p + 8]
        pieces.append(piece + bias_ref[...])
    rebuilt = jnp.concatenate(pieces, axis=0)
    recon_ref[...] = rebuilt[:local].astype(bf16)
    residual = (rebuilt - acts_ref[...]).astype(bf16)
    right_ref[...] = (residual.astype(f32) * (A * 2.0 / total_rows)).astype(bf16)
    norm = lax.rsqrt(s0[...] + s1[...] + norm_eps)
    scale = (A * sparsity_coef / total_rows) * counts_ref[...] * norm
    for q in range(scale.shape[0]):
        scale_ref[:, q * TALL:(q + 1) * TALL] = scale[q:q + 1]

    right = right_ref[...]
    eye = (
        lax.broadcasted_iota(jnp.int32, (block, block), 0)
        == lax.broadcasted_iota(jnp.int32, (block, block), 1)
    )

    @pl.loop(0, steps)
    def _(i):
        for copy in loads(i):
            copy.wait()

        @pl.when(i >= out_slots)
        def _():
            store(i - out_slots).wait()

        m_ref, v_ref = m_buf.at[lax.rem(i, slots)], v_buf.at[lax.rem(i, slots)]
        out_ref = out_buf.at[lax.rem(i, out_slots)]
        for b in range(tall // block):
            here = pl.ds(b * block, block)
            there = pl.ds(pl.multiple_of(i * tall + b * block, block), block)
            diag = jnp.where(eye, scale_ref[:, there], 0.0).astype(bf16)
            left = jnp.concatenate([diag, act_ref[:, there].T], axis=1)
            for c in range(0, depth, 256):
                cols = slice(c, min(c + 256, depth))
                both = jnp.concatenate([w_ref[there, cols], right[:, cols]], axis=0)
                g = jnp.dot(left, both, preferred_element_type=f32)
                x = v_ref[here, cols].astype(f32) + g * g
                r = lax.rsqrt(x)
                top = (m_ref[here, cols].astype(f32) + K * g) * r
                step = top * pltpu.reciprocal(E * r + 1.0 / C, approx=True)
                out_ref[here, cols] = step.astype(bf16)
        store(i).start()

        @pl.when(i + slots < steps)
        def _():
            for copy in loads(i + slots):
                copy.start()

    for i in range(steps - out_slots, steps):
        store(i).wait()


def adam(acts, mine, others, bias, act, counts, sums, w, m, v, local, tall=TALL, block=128):
    width, depth = w.shape
    total = mine.shape[0]
    slots, out_slots = 3, 2
    return pl.pallas_call(
        functools.partial(adam_kernel, tall, block),
        in_specs=[VM] * 11 + [HBM, HBM],
        out_specs=[VM, HBM],
        out_shape=[
            jax.ShapeDtypeStruct((local, depth), bf16),
            pltpu.HBM((width, depth), bf16),
        ],
        scratch_shapes=[
            pltpu.VMEM((total, depth), bf16),
            pltpu.VMEM((1, width), f32),
            pltpu.VMEM((slots, tall, depth), bf16),
            pltpu.VMEM((slots, tall, depth), bf16),
            pltpu.VMEM((out_slots, tall, depth), bf16),
            pltpu.SemaphoreType.DMA((slots,)),
            pltpu.SemaphoreType.DMA((slots,)),
            pltpu.SemaphoreType.DMA((out_slots,)),
        ],
        compiler_params=params(21),
        cost_estimate=cost(8 * total * w.size, 6 * w.size),
        name="adam",
    )(
        acts, mine, *others, bias, act, counts, *sums, w,
        pltpu.with_memory_space_constraint(m, pltpu.HBM),
        pltpu.with_memory_space_constraint(v, pltpu.HBM),
    )


def fast(sizes, activations, enc_weight, enc_bias, dec_weight, dec_bias, first_moment, second_moment):
    feat = sizes[0]
    parts = sizes[1] * sizes[2]
    local = activations.shape[0]
    me = place(PARTS, sizes[1:]).astype(jnp.int32).reshape(1)
    near = swap(activations, "feat", feat, 1)
    mine, bias = widen(activations, dec_bias.reshape(1, -1))
    near, mine = lax.optimization_barrier((near, mine))
    pair = join(mine, near)
    rows = [pair] + [swap(pair, "feat", feat, k) for k in (2, 4, 6)]
    w3, w1 = fetch((3, 1), me, enc_weight, pair, parts)
    all_rows, x = center(rows, bias)
    x, w3, w1 = lax.optimization_barrier((x, w3, w1))
    p3, w2 = encode(me, x, w3, enc_weight, ahead=2)
    p1, w0 = encode(me, x, w1, enc_weight, ahead=0)
    p2 = encode(me, x, w2)
    p0 = encode(me, x, w0)
    arrived = [p0] + [swap(p, PARTS, parts, k) for k, p in ((1, p1), (2, p2), (3, p3))]

    w = pltpu.with_memory_space_constraint(dec_weight, pltpu.VMEM)
    sums = squares(w, p0)
    arrived, sums = lax.optimization_barrier((arrived, sums))
    act = activate(me, enc_bias.reshape(1, -1), arrived)
    acts = [act] + [swap(act, PARTS, parts, k) for k in range(1, parts)]
    part = rebuild_own(me, act, w)
    part, sums = lax.optimization_barrier((part, sums))
    sums = add(sums, swap(sums, PARTS, parts, 1))
    part, all_act, counts = rebuild(me, part, acts, w)
    other = swap(part, "feat", feat, 1)
    other, sums = lax.optimization_barrier((other, sums))
    part, narrow = pair_sum(part, other)
    others = [swap(narrow, "feat", feat, k) for k in (2, 4, 6)]
    sums = (sums, swap(sums, PARTS, parts, 2))
    return adam(
        all_rows, part, others, bias, all_act, counts, sums, w, first_moment, second_moment, local
    )


def plain(activations, enc_weight, enc_bias, dec_weight, dec_bias, first_moment, second_moment):
    local_rows = activations.shape[0]
    total_rows = local_rows * lax.axis_size("feat")
    centered = (activations.astype(f32) - dec_bias).astype(bf16)
    partial_value = jnp.dot(
        lax.all_gather(centered, "feat", axis=0, tiled=True), enc_weight, preferred_element_type=f32
    )
    wide = dec_weight.astype(f32)
    squares_sum = jnp.sum(wide * wide, axis=1)
    pre_sum, sum_squares = lax.psum((partial_value, squares_sum), PARTS)
    active = jnp.maximum(pre_sum + enc_bias, 0.0).astype(bf16)
    part = jnp.dot(active, dec_weight, preferred_element_type=f32)
    rebuilt = lax.psum_scatter(part, "feat", scatter_dimension=0, tiled=True) + dec_bias
    residual = (rebuilt - activations.astype(f32)).astype(bf16)
    all_residual = lax.all_gather(residual, "feat", axis=0, tiled=True)
    product = lax.dot_general(
        active, all_residual, (((0,), (0,)), ((), ())), preferred_element_type=f32
    )
    counts = jnp.sum(active.astype(f32), axis=0)
    row_norm = jnp.sqrt(sum_squares + norm_eps)
    gradient = (
        2.0 / total_rows * product
        + sparsity_coef / total_rows * counts[:, None] * wide / row_norm[:, None]
    )
    moment_one = beta_one * first_moment.astype(f32) + (1.0 - beta_one) * gradient
    moment_two = beta_two * second_moment.astype(f32) + (1.0 - beta_two) * gradient * gradient
    dec_step = moment_one / bias_one / (jnp.sqrt(moment_two / bias_two) + adam_eps)
    return rebuilt.astype(bf16), dec_step.astype(bf16)


def solution(mesh):
    sizes = tuple(mesh.shape[name] for name in ("feat", "row", "rep"))

    def shards(*args):
        local, depth = args[0].shape
        width = args[1].shape[1]
        fits = sizes[0] == 8 and local == 4 and depth % 128 == 0
        if fits and width % (TALL * sizes[1] * sizes[2]) == 0 and sizes[1] * sizes[2] == 4:
            return fast(sizes, *args)
        return plain(*args)

    split = P("feat", PARTS)
    return jax.shard_map(
        shards,
        mesh=mesh,
        in_specs=(split, P(PARTS, "feat"), P("feat"), split, P(PARTS), split, split),
        out_specs=(split, split),
        check_vma=False,
    )
```

time: 106 us -> 76.7 us (0.72)
  waiting for transfers between devices: 20 us -> 9.6 us
  Pallas kernels: 54.4 us -> 44.1 us
  local copies, waits for them, and re-layouts: 7.83 us -> 1.46 us
  starting transfers between devices: 21.7 us -> 20.5 us
    ppermute x17 -> x16, waiting for transfers between devices: 20 us -> 9.6 us  [swap(): return lax.ppermute(x, axis, [(a, a ^ k) for a in range(n)])]
    pallas_call x3 -> x12, Pallas kernels: 50.1 us -> 40.7 us  [the longest x1 23.4 us: adam(): pl.pallas_call(functools.partial(adam_kernel, tall, block), in_specs=[VM]...]
    unnamed x6 -> x14, local copies, waits for them, and re-layouts: 7.13 us -> 0.76 us
    ppermute x17 -> x16, starting transfers between devices: 21.7 us -> 20.5 us  [swap(): return lax.ppermute(x, axis, [(a, a ^ k) for a in range(n)])]
  transfers between devices with their start and end apart: 17 -> 16, of which waited for: 10 -> 6; matrix products, arithmetic and copies ran while one was open for 1% -> 1% of each run, Pallas kernels for 9% -> 14%
where the time goes in v2:
time: 76.7 us; the launch traced here: 76.5 us
  Pallas kernels  44.1 us (57%)
  starting transfers between devices  20.5 us (27%)
  waiting for transfers between devices  9.6 us (13%)
  local copies, waits for them, and re-layouts  1.46 us (2%)
  between operations  0.85 us (1%)
    pallas_call x1, Pallas kernels, adam(): pl.pallas_call(functools.partial(adam_kernel, tall, block), in_specs=[VM]...  23.4 us
    ppermute x16, starting transfers between devices, swap(): return lax.ppermute(x, axis, [(a, a ^ k) for a in range(n)])  20.5 us
    ppermute x16, waiting for transfers between devices, swap(): return lax.ppermute(x, axis, [(a, a ^ k) for a in range(n)])  9.6 us
    pallas_call x4, Pallas kernels, encode(): pl.pallas_call(functools.partial(encode_kernel, ahead), in_specs=[pl.Bloc...  8.21 us
    pallas_call x1, Pallas kernels, squares(): pl.pallas_call(squares_kernel, in_specs=[VM, ANY], out_specs=VM, out_shap...  4.26 us
    pallas_call x1, Pallas kernels, fetch(): pl.pallas_call(functools.partial(fetch_kernel, ks), in_specs=[pl.BlockSpe...  3.8 us
    pallas_call x1, Pallas kernels, rebuild(): pl.pallas_call(rebuild_kernel, in_specs=[pl.BlockSpec(memory_space=pltpu....  3.27 us
  transfers between devices with their start and end apart: 16, of which 6 were waited for; matrix products, arithmetic and copies ran while one was open for 1% of the time, Pallas kernels for 14%

profile of v2, /device:TPU:0, one launch (start us, length us, event | category | flops | bytes accessed | tf_op | source)
XLA Modules:
  0.0 76.5 jit_solution(10603403832424196793)
XLA Ops:
  1.1 0.7 reshape.13.bias_ref
  1.9 0.7 copy-done.1
  2.6 4.7 %collective-permute-start.3 = (f32[8,1152]{1,0:T(8,128)S(1)}, f32[8,1152]{1,0:T(8,128)S(1)}, u32[]{:S(2)}, u32[]{:S(2)}) collective-permute-start(f32[8,1152]{1,0:T(8,128)S(1)} %join.1.refs_0_._), channel_id=1, source_target_pairs={{0,24},{4,28},{8,16},{12,20},{16,8},{20,12},{24,0},{28,4},{1,25},{... | collective-permute-start | bytes 110600 | tf_op jit(solution)/shard_map/ppermute | solution.py:42
  7.9 3.8 %fetch.1 = (bf16[1152,2048]{1,0:T(8,128)(2,1)S(1)}, bf16[1152,2048]{1,0:T(8,128)(2,1)S(1)}) custom-call(s32[1]{0:T(128)} %bitcast.me_ref, bf16[1152,8192]{1,0:T(8,128)(2,1)} %refs_0_.3, f32[8,1152]{1,0:T(8,128)S(1)} %join.1.refs_0_._), custom_call_target="tpu_custom_call" | custom-call | bytes 9437184 | tf_op jit(solution)/shard_map/fetch/pallas_call | solution.py:135
  12.2 2.5 %encode.4 = (bf16[32,2048]{1,0:T(8,128)(2,1)S(1)}, bf16[1152,2048]{1,0:T(8,128)(2,1)S(1)}) custom-call(s32[1]{0:T(128)} %bitcast.me_ref, bf16[32,1152]{1,0:T(8,128)(2,1)S(1)} %get-tuple-element.39.x_ref, bf16[1152,2048]{1,0:T(8,128)(2,1)S(1)} %get-tuple-element.40.here_ref, bf16[1152,8192]{1,0:T(8,128)(2,1)} %refs_0_.3), custom_call_target="tpu_custom_call" | custom-call | flops 150994944 | bytes 4718592 | tf_op jit(solution)/shard_map/encode/pallas_call | solution.py:172
  14.7 3.2 %encode.6 = (bf16[32,2048]{1,0:T(8,128)(2,1)S(1)}, bf16[1152,2048]{1,0:T(8,128)(2,1)S(1)}) custom-call(s32[1]{0:T(128)} %bitcast.me_ref, bf16[32,1152]{1,0:T(8,128)(2,1)S(1)} %get-tuple-element.39.x_ref, bf16[1152,2048]{1,0:T(8,128)(2,1)S(1)} %get-tuple-element.43.here_ref, bf16[1152,8192]{1,0:T(8,128)(2,1)} %refs_0_.3), custom_call_target="tpu_custom_call" | custom-call | flops 150994944 | bytes 4718592 | tf_op jit(solution)/shard_map/encode/pallas_call | solution.py:172
  17.9 1.3 %encode.7 = bf16[32,2048]{1,0:T(8,128)(2,1)S(1)} custom-call(s32[1]{0:T(128)} %bitcast.me_ref, bf16[32,1152]{1,0:T(8,128)(2,1)S(1)} %get-tuple-element.39.x_ref, bf16[1152,2048]{1,0:T(8,128)(2,1)S(1)} %get-tuple-element.44.here_ref), custom_call_target="tpu_custom_call" | custom-call | flops 150994944 | bytes 4718592 | tf_op jit(solution)/shard_map/encode/pallas_call | solution.py:172
  19.2 1.5 %collective-permute-start.5 = (bf16[32,2048]{1,0:T(8,128)(2,1)S(1)}, bf16[32,2048]{1,0:T(8,128)(2,1)S(1)}, u32[]{:S(2)}, u32[]{:S(2)}) collective-permute-start(bf16[32,2048]{1,0:T(8,128)(2,1)S(1)} %encode.7), channel_id=1, source_target_pairs={{0,2},{1,3},{2,0},{3,1},{4,6},{5,7},{6,4},{7,5},{8,10},{9,11},{10,... | collective-permute-start | bytes 393224 | tf_op jit(solution)/shard_map/ppermute | solution.py:42
  20.7 1.4 %collective-permute-start.6 = (bf16[32,2048]{1,0:T(8,128)(2,1)S(1)}, bf16[32,2048]{1,0:T(8,128)(2,1)S(1)}, u32[]{:S(2)}, u32[]{:S(2)}) collective-permute-start(bf16[32,2048]{1,0:T(8,128)(2,1)S(1)} %get-tuple-element.45), channel_id=1, source_target_pairs={{0,3},{1,2},{2,1},{3,0},{4,7},{5,6},{6,5},{7,4},{8,11},{9,10},{10,... | collective-permute-start | bytes 393224 | tf_op jit(solution)/shard_map/ppermute | solution.py:42
  22.7 1.3 %encode.5._.refs_0_ = bf16[32,2048]{1,0:T(8,128)(2,1)S(1)} custom-call(s32[1]{0:T(128)} %bitcast.me_ref, bf16[32,1152]{1,0:T(8,128)(2,1)S(1)} %get-tuple-element.39.x_ref, bf16[1152,2048]{1,0:T(8,128)(2,1)S(1)} %get-tuple-element.41.here_ref), custom_call_target="tpu_custom_call" | custom-call | flops 150994944 | bytes 4718592 | tf_op jit(solution)/shard_map/encode/pallas_call | solution.py:172
  24.0 4.3 %squares.1.a_ref = f32[8,1024]{1,0:T(8,128)S(1)} custom-call(bf16[8192,1152]{1,0:T(8,128)(2,1)S(1)} %bitcast.3, bf16[32,2048]{1,0:T(8,128)(2,1)S(1)} %encode.5._.refs_0_), custom_call_target="tpu_custom_call" | custom-call | flops 18874368 | bytes 18874368 | tf_op jit(solution)/shard_map/squares/pallas_call | solution.py:220
  28.4 2.5 %collective-permute-start.9 = (bf16[32,2048]{1,0:T(8,128)(2,1)S(1)}, bf16[32,2048]{1,0:T(8,128)(2,1)S(1)}, u32[]{:S(2)}, u32[]{:S(2)}) collective-permute-start(bf16[32,2048]{1,0:T(8,128)(2,1)S(1)} %activate.1.act_ref.refs_0_), channel_id=1, source_target_pairs={{0,3},{1,2},{2,1},{3,0},{4,7},{5,6},{6,5},{7,4},{8,11},{9,10},{10,... | collective-permute-start | bytes 393224 | tf_op jit(solution)/shard_map/ppermute | solution.py:42
  32.0 1.1 %rebuild_own.1.part_ref = f32[32,1152]{1,0:T(8,128)S(1)} custom-call(s32[1]{0:T(128)} %bitcast.me_ref, bf16[32,2048]{1,0:T(8,128)(2,1)S(1)} %activate.1.act_ref.refs_0_, bf16[8192,1152]{1,0:T(8,128)(2,1)S(1)} %bitcast.3), custom_call_target="tpu_custom_call" | custom-call | flops 150994944 | bytes 4718592 | tf_op jit(solution)/shard_map/rebuild_own/pallas_call | solution.py:267
  33.0 2.5 %collective-permute-done.9.refs_3_ = bf16[32,2048]{1,0:T(8,128)(2,1)S(1)} collective-permute-done((bf16[32,2048]{1,0:T(8,128)(2,1)S(1)}, bf16[32,2048]{1,0:T(8,128)(2,1)S(1)}, u32[]{:S(2)}, u32[]{:S(2)}) %collective-permute-start.9) | collective-permute-done | bytes 131104 | tf_op jit(solution)/shard_map/ppermute | solution.py:42
  35.6 0.9 %collective-permute-done.8.refs_2_ = bf16[32,2048]{1,0:T(8,128)(2,1)S(1)} collective-permute-done((bf16[32,2048]{1,0:T(8,128)(2,1)S(1)}, bf16[32,2048]{1,0:T(8,128)(2,1)S(1)}, u32[]{:S(2)}, u32[]{:S(2)}) %collective-permute-start.8) | collective-permute-done | bytes 131104 | tf_op jit(solution)/shard_map/ppermute | solution.py:42
  36.4 3.3 %rebuild.1 = (f32[32,1152]{1,0:T(8,128)S(1)}, bf16[32,8192]{1,0:T(8,128)(2,1)S(1)}, f32[8,1024]{1,0:T(8,128)S(1)}) custom-call(s32[1]{0:T(128)} %bitcast.me_ref, f32[32,1152]{1,0:T(8,128)S(1)} %rebuild_own.1.part_ref, bf16[32,2048]{1,0:T(8,128)(2,1)S(1)} %activate.1.act_ref.refs_0_, bf16[32,2048]{1,0:T(8,128)(2,1)S(1)} %collective-permute-done.7.refs_1_, ...), custom_call_target="tpu_custom_call" | custom-call | flops 603979776 | bytes 18874368 | tf_op jit(solution)/shard_map/rebuild/pallas_call | solution.py:280
  39.8 1.5 %collective-permute-start.11 = (f32[8,1024]{1,0:T(8,128)S(1)}, f32[8,1024]{1,0:T(8,128)S(1)}, u32[]{:S(2)}, u32[]{:S(2)}) collective-permute-start(f32[8,1024]{1,0:T(8,128)S(1)} %squares.1.a_ref), channel_id=1, source_target_pairs={{0,1},{1,0},{2,3},{3,2},{4,5},{5,4},{6,7},{7,6},{8,9},{9,8},{10,11... | collective-permute-start | bytes 98312 | tf_op jit(solution)/shard_map/ppermute | solution.py:42
  41.3 2.4 %collective-permute-done.11.b_ref = f32[8,1024]{1,0:T(8,128)S(1)} collective-permute-done((f32[8,1024]{1,0:T(8,128)S(1)}, f32[8,1024]{1,0:T(8,128)S(1)}, u32[]{:S(2)}, u32[]{:S(2)}) %collective-permute-start.11) | collective-permute-done | bytes 32800 | tf_op jit(solution)/shard_map/ppermute | solution.py:42
  43.8 3.5 %collective-permute-start.14 = (bf16[32,1152]{1,0:T(8,128)(2,1)S(1)}, bf16[32,1152]{1,0:T(8,128)(2,1)S(1)}, u32[]{:S(2)}, u32[]{:S(2)}) collective-permute-start(bf16[32,1152]{1,0:T(8,128)(2,1)S(1)} %get-tuple-element.56), channel_id=1, source_target_pairs={{0,24},{4,28},{8,16},{12,20},{16,8},{20,12},{24,0},{28,4},{1,25},{... | collective-permute-start | bytes 221192 | tf_op jit(solution)/shard_map/ppermute | solution.py:42
  47.3 0.9 %collective-permute-start.12 = (bf16[32,1152]{1,0:T(8,128)(2,1)S(1)}, bf16[32,1152]{1,0:T(8,128)(2,1)S(1)}, u32[]{:S(2)}, u32[]{:S(2)}) collective-permute-start(bf16[32,1152]{1,0:T(8,128)(2,1)S(1)} %get-tuple-element.56), channel_id=1, source_target_pairs={{0,8},{4,12},{8,0},{12,4},{16,24},{20,28},{24,16},{28,20},{1,9},{5... | collective-permute-start | bytes 221192 | tf_op jit(solution)/shard_map/ppermute | solution.py:42
  48.3 1.5 %collective-permute-start.15 = (f32[8,1024]{1,0:T(8,128)S(1)}, f32[8,1024]{1,0:T(8,128)S(1)}, u32[]{:S(2)}, u32[]{:S(2)}) collective-permute-start(f32[8,1024]{1,0:T(8,128)S(1)} %add.5.s0), channel_id=1, source_target_pairs={{0,2},{1,3},{2,0},{3,1},{4,6},{5,7},{6,4},{7,5},{8,10},{9,11},{10,... | collective-permute-start | bytes 98312 | tf_op jit(solution)/shard_map/ppermute | solution.py:42
  49.8 2.4 %collective-permute-done.15.s1 = f32[8,1024]{1,0:T(8,128)S(1)} collective-permute-done((f32[8,1024]{1,0:T(8,128)S(1)}, f32[8,1024]{1,0:T(8,128)S(1)}, u32[]{:S(2)}, u32[]{:S(2)}) %collective-permute-start.15) | collective-permute-done | bytes 32800 | tf_op jit(solution)/shard_map/ppermute | solution.py:42
  52.2 0.9 %collective-permute-done.13.o2 = bf16[32,1152]{1,0:T(8,128)(2,1)S(1)} collective-permute-done((bf16[32,1152]{1,0:T(8,128)(2,1)S(1)}, bf16[32,1152]{1,0:T(8,128)(2,1)S(1)}, u32[]{:S(2)}, u32[]{:S(2)}) %collective-permute-start.13) | collective-permute-done | bytes 73760 | tf_op jit(solution)/shard_map/ppermute | solution.py:42
  53.1 23.4 %adam.1 = (bf16[4,1152]{1,0:T(4,128)(2,1)}, bf16[8192,1152]{1,0:T(8,128)(2,1)}) custom-call(f32[32,1152]{1,0:T(8,128)S(1)} %get-tuple-element.35.acts_ref, f32[32,1152]{1,0:T(8,128)S(1)} %get-tuple-element.55.mine_ref, bf16[32,1152]{1,0:T(8,128)(2,1)S(1)} %collective-permute-done.12.o1, bf16[32,1152]{1,0:T(8,128)(2,1)S(1)} %collective-permute-done.13.o2, ...), custom_call_target="tpu_custom_call" | custom-call | flops 2415919104 | bytes 56623104 | tf_op jit(solution)/shard_map/adam/pallas_call | solution.py:421
  (39 shorter events, 3.5 us)
Async XLA Ops:
  0.6 1.9 %collective-permute-start = (bf16[4,1152]{1,0:T(4,128)(2,1)}, bf16[4,1152]{1,0:T(4,128)(2,1)S(1)}, u32[]{:S(2)}, u32[]{:S(2)}) collective-permute-start(bf16[4,1152]{1,0:T(4,128)(2,1)} %x_ref.1), channel_id=1, source_target_pairs={{0,4},{4,0},{8,12},{12,8},{16,20},{20,16},{24,28},{28,24},{1,5},{5... | collective-permute-start | bytes 27656 | tf_op jit(solution)/shard_map/ppermute | solution.py:42
  1.8 0.7 copy-start.1
  2.6 9.1 %collective-permute-start.3 = (f32[8,1152]{1,0:T(8,128)S(1)}, f32[8,1152]{1,0:T(8,128)S(1)}, u32[]{:S(2)}, u32[]{:S(2)}) collective-permute-start(f32[8,1152]{1,0:T(8,128)S(1)} %join.1.refs_0_._), channel_id=1, source_target_pairs={{0,24},{4,28},{8,16},{12,20},{16,8},{20,12},{24,0},{28,4},{1,25},{... | collective-permute-start | bytes 110600 | tf_op jit(solution)/shard_map/ppermute | solution.py:42
  7.2 4.9 %collective-permute-start.2 = (f32[8,1152]{1,0:T(8,128)S(1)}, f32[8,1152]{1,0:T(8,128)S(1)}, u32[]{:S(2)}, u32[]{:S(2)}) collective-permute-start(f32[8,1152]{1,0:T(8,128)S(1)} %join.1.refs_0_._), channel_id=1, source_target_pairs={{0,16},{4,20},{8,24},{12,28},{16,0},{20,4},{24,8},{28,12},{1,17},{... | collective-permute-start | bytes 110600 | tf_op jit(solution)/shard_map/ppermute | solution.py:42
  7.2 4.9 %collective-permute-start.1 = (f32[8,1152]{1,0:T(8,128)S(1)}, f32[8,1152]{1,0:T(8,128)S(1)}, u32[]{:S(2)}, u32[]{:S(2)}) collective-permute-start(f32[8,1152]{1,0:T(8,128)S(1)} %join.1.refs_0_._), channel_id=1, source_target_pairs={{0,8},{4,12},{8,0},{12,4},{16,24},{20,28},{24,16},{28,20},{1,9},{5... | collective-permute-start | bytes 110600 | tf_op jit(solution)/shard_map/ppermute | solution.py:42
  12.1 11.8 %slice-start = ((s8[18874368]{0:T(1024)(128)(4,1)}), s8[4194304]{0:T(1024)(128)(4,1)S(1)}, s32[]{:S(2)}) async-start(s8[18874368]{0:T(1024)(128)(4,1)} %bitcast.2), calls=%async_computation | async-start | bytes 8388608
  12.1 11.8 %slice-start.1 = ((s8[18874368]{0:T(1024)(128)(4,1)}), s8[4194304]{0:T(1024)(128)(4,1)S(1)}, s32[]{:S(2)}) async-start(s8[18874368]{0:T(1024)(128)(4,1)} %bitcast.2), calls=%async_computation.1 | async-start | bytes 8388608
  12.2 11.8 %slice-start.2 = ((s8[18874368]{0:T(1024)(128)(4,1)}), s8[4194304]{0:T(1024)(128)(4,1)S(1)}, s32[]{:S(2)}) async-start(s8[18874368]{0:T(1024)(128)(4,1)} %bitcast.2), calls=%async_computation.2 | async-start | bytes 8388608
  14.7 9.3 %slice-start.3 = ((s8[18874368]{0:T(1024)(128)(4,1)}), s8[4194304]{0:T(1024)(128)(4,1)S(1)}, s32[]{:S(2)}) async-start(s8[18874368]{0:T(1024)(128)(4,1)} %bitcast.2), calls=%async_computation.3 | async-start | bytes 8388608
  14.7 9.3 %slice-start.4 = ((s8[18874368]{0:T(1024)(128)(4,1)}), s8[2097152]{0:T(1024)(128)(4,1)S(1)}, s32[]{:S(2)}) async-start(s8[18874368]{0:T(1024)(128)(4,1)} %bitcast.2), calls=%async_computation.4 | async-start | bytes 4194304
  17.9 10.4 %copy-start = (f32[8192]{0:T(1024)S(1)}, f32[8192]{0:T(1024)}, u32[]{:S(2)}) copy-start(f32[8192]{0:T(1024)} %param.9) | copy-start | bytes 98308
  19.2 9.1 %collective-permute-start.5 = (bf16[32,2048]{1,0:T(8,128)(2,1)S(1)}, bf16[32,2048]{1,0:T(8,128)(2,1)S(1)}, u32[]{:S(2)}, u32[]{:S(2)}) collective-permute-start(bf16[32,2048]{1,0:T(8,128)(2,1)S(1)} %encode.7), channel_id=1, source_target_pairs={{0,2},{1,3},{2,0},{3,1},{4,6},{5,7},{6,4},{7,5},{8,10},{9,11},{10,... | collective-permute-start | bytes 393224 | tf_op jit(solution)/shard_map/ppermute | solution.py:42
  20.7 7.6 %collective-permute-start.6 = (bf16[32,2048]{1,0:T(8,128)(2,1)S(1)}, bf16[32,2048]{1,0:T(8,128)(2,1)S(1)}, u32[]{:S(2)}, u32[]{:S(2)}) collective-permute-start(bf16[32,2048]{1,0:T(8,128)(2,1)S(1)} %get-tuple-element.45), channel_id=1, source_target_pairs={{0,3},{1,2},{2,1},{3,0},{4,7},{5,6},{6,5},{7,4},{8,11},{9,10},{10,... | collective-permute-start | bytes 393224 | tf_op jit(solution)/shard_map/ppermute | solution.py:42
  22.2 6.2 %collective-permute-start.4 = (bf16[32,2048]{1,0:T(8,128)(2,1)S(1)}, bf16[32,2048]{1,0:T(8,128)(2,1)S(1)}, u32[]{:S(2)}, u32[]{:S(2)}) collective-permute-start(bf16[32,2048]{1,0:T(8,128)(2,1)S(1)} %get-tuple-element.42), channel_id=1, source_target_pairs={{0,1},{1,0},{2,3},{3,2},{4,5},{5,4},{6,7},{7,6},{8,9},{9,8},{10,11... | collective-permute-start | bytes 393224 | tf_op jit(solution)/shard_map/ppermute | solution.py:42
  28.4 7.1 %collective-permute-start.9 = (bf16[32,2048]{1,0:T(8,128)(2,1)S(1)}, bf16[32,2048]{1,0:T(8,128)(2,1)S(1)}, u32[]{:S(2)}, u32[]{:S(2)}) collective-permute-start(bf16[32,2048]{1,0:T(8,128)(2,1)S(1)} %activate.1.act_ref.refs_0_), channel_id=1, source_target_pairs={{0,3},{1,2},{2,1},{3,0},{4,7},{5,6},{6,5},{7,4},{8,11},{9,10},{10,... | collective-permute-start | bytes 393224 | tf_op jit(solution)/shard_map/ppermute | solution.py:42
  30.9 5.5 %collective-permute-start.8 = (bf16[32,2048]{1,0:T(8,128)(2,1)S(1)}, bf16[32,2048]{1,0:T(8,128)(2,1)S(1)}, u32[]{:S(2)}, u32[]{:S(2)}) collective-permute-start(bf16[32,2048]{1,0:T(8,128)(2,1)S(1)} %activate.1.act_ref.refs_0_), channel_id=1, source_target_pairs={{0,2},{1,3},{2,0},{3,1},{4,6},{5,7},{6,4},{7,5},{8,10},{9,11},{10,... | collective-permute-start | bytes 393224 | tf_op jit(solution)/shard_map/ppermute | solution.py:42
  31.4 5.0 %collective-permute-start.7 = (bf16[32,2048]{1,0:T(8,128)(2,1)S(1)}, bf16[32,2048]{1,0:T(8,128)(2,1)S(1)}, u32[]{:S(2)}, u32[]{:S(2)}) collective-permute-start(bf16[32,2048]{1,0:T(8,128)(2,1)S(1)} %activate.1.act_ref.refs_0_), channel_id=1, source_target_pairs={{0,1},{1,0},{2,3},{3,2},{4,5},{5,4},{6,7},{7,6},{8,9},{9,8},{10,11... | collective-permute-start | bytes 393224 | tf_op jit(solution)/shard_map/ppermute | solution.py:42
  39.7 4.1 %collective-permute-start.10 = (f32[32,1152]{1,0:T(8,128)S(1)}, f32[32,1152]{1,0:T(8,128)S(1)}, u32[]{:S(2)}, u32[]{:S(2)}) collective-permute-start(f32[32,1152]{1,0:T(8,128)S(1)} %get-tuple-element.52.mine_ref), channel_id=1, source_target_pairs={{0,4},{4,0},{8,12},{12,8},{16,20},{20,16},{24,28},{28,24},{1,5},{5... | collective-permute-start | bytes 442376 | tf_op jit(solution)/shard_map/ppermute | solution.py:42
  39.8 4.0 %collective-permute-start.11 = (f32[8,1024]{1,0:T(8,128)S(1)}, f32[8,1024]{1,0:T(8,128)S(1)}, u32[]{:S(2)}, u32[]{:S(2)}) collective-permute-start(f32[8,1024]{1,0:T(8,128)S(1)} %squares.1.a_ref), channel_id=1, source_target_pairs={{0,1},{1,0},{2,3},{3,2},{4,5},{5,4},{6,7},{7,6},{8,9},{9,8},{10,11... | collective-permute-start | bytes 98312 | tf_op jit(solution)/shard_map/ppermute | solution.py:42
  43.8 8.4 %collective-permute-start.14 = (bf16[32,1152]{1,0:T(8,128)(2,1)S(1)}, bf16[32,1152]{1,0:T(8,128)(2,1)S(1)}, u32[]{:S(2)}, u32[]{:S(2)}) collective-permute-start(bf16[32,1152]{1,0:T(8,128)(2,1)S(1)} %get-tuple-element.56), channel_id=1, source_target_pairs={{0,24},{4,28},{8,16},{12,20},{16,8},{20,12},{24,0},{28,4},{1,25},{... | collective-permute-start | bytes 221192 | tf_op jit(solution)/shard_map/ppermute | solution.py:42
  47.3 5.8 %collective-permute-start.13 = (bf16[32,1152]{1,0:T(8,128)(2,1)S(1)}, bf16[32,1152]{1,0:T(8,128)(2,1)S(1)}, u32[]{:S(2)}, u32[]{:S(2)}) collective-permute-start(bf16[32,1152]{1,0:T(8,128)(2,1)S(1)} %get-tuple-element.56), channel_id=1, source_target_pairs={{0,16},{4,20},{8,24},{12,28},{16,0},{20,4},{24,8},{28,12},{1,17},{... | collective-permute-start | bytes 221192 | tf_op jit(solution)/shard_map/ppermute | solution.py:42
  47.3 5.8 %collective-permute-start.12 = (bf16[32,1152]{1,0:T(8,128)(2,1)S(1)}, bf16[32,1152]{1,0:T(8,128)(2,1)S(1)}, u32[]{:S(2)}, u32[]{:S(2)}) collective-permute-start(bf16[32,1152]{1,0:T(8,128)(2,1)S(1)} %get-tuple-element.56), channel_id=1, source_target_pairs={{0,8},{4,12},{8,0},{12,4},{16,24},{20,28},{24,16},{28,20},{1,9},{5... | collective-permute-start | bytes 221192 | tf_op jit(solution)/shard_map/ppermute | solution.py:42
  48.3 3.9 %collective-permute-start.15 = (f32[8,1024]{1,0:T(8,128)S(1)}, f32[8,1024]{1,0:T(8,128)S(1)}, u32[]{:S(2)}, u32[]{:S(2)}) collective-permute-start(f32[8,1024]{1,0:T(8,128)S(1)} %add.5.s0), channel_id=1, source_target_pairs={{0,2},{1,3},{2,0},{3,1},{4,6},{5,7},{6,4},{7,5},{8,10},{9,11},{10,... | collective-permute-start | bytes 98312 | tf_op jit(solution)/shard_map/ppermute | solution.py:42

commit v3 on v2

--- a/solution.py
+++ b/solution.py
@@ -330,7 +330,7 @@
 
 
 def adam_kernel(tall, block, acts_ref, mine_ref, o1, o2, o3, bias_ref, act_ref, counts_ref, s0, s1,
-                w_ref, m_hbm, v_hbm, recon_ref, out_hbm, right_ref, scale_ref, m_buf, v_buf, out_buf,
+                w_ref, m0_ref, v0_ref, m_hbm, v_hbm, recon_ref, out_hbm, right_ref, scale_ref, m_buf, v_buf, out_buf,
                 m_sems, v_sems, out_sems):
     total_rows, depth = mine_ref.shape
     local = recon_ref.shape[0]
@@ -351,7 +351,8 @@
         slot = lax.rem(i, out_slots)
         return pltpu.make_async_copy(out_buf.at[slot], tile(out_hbm, i), out_sems.at[slot])
 
-    for i in range(slots):
+    early = m0_ref.shape[0] // tall
+    for i in range(early, early + slots):
         for copy in loads(i):
             copy.start()
 
@@ -378,16 +379,7 @@
         == lax.broadcasted_iota(jnp.int32, (block, block), 1)
     )
 
-    @pl.loop(0, steps)
-    def _(i):
-        for copy in loads(i):
-            copy.wait()
-
-        @pl.when(i >= out_slots)
-        def _():
-            store(i - out_slots).wait()
-
-        m_ref, v_ref = m_buf.at[lax.rem(i, slots)], v_buf.at[lax.rem(i, slots)]
+    def compute(i, m_ref, v_ref):
         out_ref = out_buf.at[lax.rem(i, out_slots)]
         for b in range(tall // block):
             here = pl.ds(b * block, block)
@@ -405,6 +397,22 @@
                 out_ref[here, cols] = step.astype(bf16)
         store(i).start()
 
+    @pl.loop(0, early)
+    def _(i):
+        compute(i, tile(m0_ref, i), tile(v0_ref, i))
+
+    @pl.loop(early, steps)
+    def _(i):
+        for copy in loads(i):
+            copy.wait()
+
+        @pl.when(i >= out_slots)
+        def _():
+            store(i - out_slots).wait()
+
+        slot = lax.rem(i, slots)
+        compute(i, m_buf.at[slot], v_buf.at[slot])
+
         @pl.when(i + slots < steps)
         def _():
             for copy in loads(i + slots):
@@ -414,13 +422,44 @@
         store(i).wait()
 
 
-def adam(acts, mine, others, bias, act, counts, sums, w, m, v, local, tall=TALL, block=128):
+def fill_kernel(m_hbm, v_hbm, _, m_ref, v_ref, sems):
+    rows = m_ref.shape[0] // PIECES
+    copies = []
+    for p in range(PIECES):
+        s = pl.ds(p * rows, rows)
+        copies.append(pltpu.make_async_copy(m_hbm.at[s], m_ref.at[s], sems.at[0, p]))
+        copies.append(pltpu.make_async_copy(v_hbm.at[s], v_ref.at[s], sems.at[1, p]))
+    for copy in copies:
+        copy.start()
+    for copy in copies:
+        copy.wait()
+
+
+def fill(rows, m, v, after):
+    out = pltpu.VMEM((rows, m.shape[1]), bf16)
+    return pl.pallas_call(
+        fill_kernel,
+        in_specs=[HBM, HBM, ANY],
+        out_specs=[VM, VM],
+        out_shape=[out, out],
+        scratch_shapes=[pltpu.SemaphoreType.DMA((2, PIECES))],
+        compiler_params=params(4),
+        cost_estimate=cost(0, 4 * rows * m.shape[1]),
+        name="fill",
+    )(
+        pltpu.with_memory_space_constraint(m, pltpu.HBM),
+        pltpu.with_memory_space_constraint(v, pltpu.HBM),
+        after,
+    )
+
+
+def adam(acts, mine, others, bias, act, counts, sums, w, first, m, v, local, tall=TALL, block=128):
     width, depth = w.shape
     total = mine.shape[0]
     slots, out_slots = 3, 2
     return pl.pallas_call(
         functools.partial(adam_kernel, tall, block),
-        in_specs=[VM] * 11 + [HBM, HBM],
+        in_specs=[VM] * 13 + [HBM, HBM],
         out_specs=[VM, HBM],
         out_shape=[
             jax.ShapeDtypeStruct((local, depth), bf16),
@@ -440,7 +479,7 @@
         cost_estimate=cost(8 * total * w.size, 6 * w.size),
         name="adam",
     )(
-        acts, mine, *others, bias, act, counts, *sums, w,
+        acts, mine, *others, bias, act, counts, *sums, w, *first,
         pltpu.with_memory_space_constraint(m, pltpu.HBM),
         pltpu.with_memory_space_constraint(v, pltpu.HBM),
     )
@@ -462,25 +501,28 @@
     p3, w2 = encode(me, x, w3, enc_weight, ahead=2)
     p1, w0 = encode(me, x, w1, enc_weight, ahead=0)
     p2 = encode(me, x, w2)
+    arrived = [swap(p, PARTS, parts, k) for k, p in ((1, p1), (2, p2), (3, p3))]
+    x, arrived[2] = lax.optimization_barrier((x, arrived[2]))
     p0 = encode(me, x, w0)
-    arrived = [p0] + [swap(p, PARTS, parts, k) for k, p in ((1, p1), (2, p2), (3, p3))]
+    arrived = [p0] + arrived
 
     w = pltpu.with_memory_space_constraint(dec_weight, pltpu.VMEM)
     sums = squares(w, p0)
     arrived, sums = lax.optimization_barrier((arrived, sums))
     act = activate(me, enc_bias.reshape(1, -1), arrived)
+    act, sums = lax.optimization_barrier((act, sums))
     acts = [act] + [swap(act, PARTS, parts, k) for k in range(1, parts)]
+    sums = add(sums, swap(sums, PARTS, parts, 1))
     part = rebuild_own(me, act, w)
-    part, sums = lax.optimization_barrier((part, sums))
-    sums = add(sums, swap(sums, PARTS, parts, 1))
+    acts, sums = lax.optimization_barrier((acts, sums))
     part, all_act, counts = rebuild(me, part, acts, w)
-    other = swap(part, "feat", feat, 1)
-    other, sums = lax.optimization_barrier((other, sums))
-    part, narrow = pair_sum(part, other)
+    part, narrow = pair_sum(part, swap(part, "feat", feat, 1))
     others = [swap(narrow, "feat", feat, k) for k in (2, 4, 6)]
     sums = (sums, swap(sums, PARTS, parts, 2))
+    first = fill(2 * TALL, first_moment, second_moment, narrow)
     return adam(
-        all_rows, part, others, bias, all_act, counts, sums, w, first_moment, second_moment, local
+        all_rows, part, others, bias, all_act, counts, sums, w, first, first_moment,
+        second_moment, local,
     )
 
 

time: 76.7 us -> 72.9 us (0.950)
  waiting for transfers between devices: 9.6 us -> 4.58 us
  Pallas kernels: 44.1 us -> 45.1 us
    ppermute x16, waiting for transfers between devices: 9.6 us -> 4.58 us  [swap(): return lax.ppermute(x, axis, [(a, a ^ k) for a in range(n)])]
    pallas_call x0 -> x1, Pallas kernels: none -> 3.78 us  [fill(): pl.pallas_call(fill_kernel, in_specs=[HBM, HBM, ANY], out_specs=[VM, VM],...]
    pallas_call x1, Pallas kernels: 23.4 us -> 21.2 us  [adam(): pl.pallas_call(functools.partial(adam_kernel, tall, block), in_specs=[VM]...]
  transfers between devices with their start and end apart: 16 -> 16, of which waited for: 6 -> 4; matrix products, arithmetic and copies ran while one was open for 1% -> 1% of each run, Pallas kernels for 14% -> 25%
where the time goes in v3:
time: 72.9 us; the launch traced here: 72.6 us
  Pallas kernels  45.1 us (62%)
  starting transfers between devices  20.5 us (28%)
  waiting for transfers between devices  4.58 us (6%)
  local copies, waits for them, and re-layouts  1.5 us (2%)
  between operations  0.94 us (1%)
    pallas_call x1, Pallas kernels, adam(): pl.pallas_call(functools.partial(adam_kernel, tall, block), in_specs=[VM]...  21.2 us
    ppermute x16, starting transfers between devices, swap(): return lax.ppermute(x, axis, [(a, a ^ k) for a in range(n)])  20.5 us
    pallas_call x4, Pallas kernels, encode(): pl.pallas_call(functools.partial(encode_kernel, ahead), in_specs=[pl.Bloc...  7.58 us
    ppermute x16, waiting for transfers between devices, swap(): return lax.ppermute(x, axis, [(a, a ^ k) for a in range(n)])  4.58 us
    pallas_call x1, Pallas kernels, squares(): pl.pallas_call(squares_kernel, in_specs=[VM, ANY], out_specs=VM, out_shap...  4.26 us
    pallas_call x1, Pallas kernels, fetch(): pl.pallas_call(functools.partial(fetch_kernel, ks), in_specs=[pl.BlockSpe...  3.8 us
    pallas_call x1, Pallas kernels, fill(): pl.pallas_call(fill_kernel, in_specs=[HBM, HBM, ANY], out_specs=[VM, VM],...  3.78 us
    pallas_call x1, Pallas kernels, rebuild(): pl.pallas_call(rebuild_kernel, in_specs=[pl.BlockSpec(memory_space=pltpu....  3.28 us
  transfers between devices with their start and end apart: 16, of which 4 were waited for; matrix products, arithmetic and copies ran while one was open for 1% of the time, Pallas kernels for 25%

profile of v3, /device:TPU:0, one launch (start us, length us, event | category | flops | bytes accessed | tf_op | source)
XLA Modules:
  0.0 72.6 jit_solution(6614388937873116161)
XLA Ops:
  1.1 0.7 reshape.13.bias_ref
  1.9 0.7 copy-done.1
  2.6 4.7 %collective-permute-start.3 = (f32[8,1152]{1,0:T(8,128)S(1)}, f32[8,1152]{1,0:T(8,128)S(1)}, u32[]{:S(2)}, u32[]{:S(2)}) collective-permute-start(f32[8,1152]{1,0:T(8,128)S(1)} %join.1.refs_0_._), channel_id=1, source_target_pairs={{0,24},{4,28},{8,16},{12,20},{16,8},{20,12},{24,0},{28,4},{1,25},{... | collective-permute-start | bytes 110600 | tf_op jit(solution)/shard_map/ppermute | solution.py:42
  7.2 0.6 collective-permute-start.1
  7.9 3.8 %fetch.1 = (bf16[1152,2048]{1,0:T(8,128)(2,1)S(1)}, bf16[1152,2048]{1,0:T(8,128)(2,1)S(1)}) custom-call(s32[1]{0:T(128)} %bitcast.me_ref, bf16[1152,8192]{1,0:T(8,128)(2,1)} %refs_0_.3, f32[8,1152]{1,0:T(8,128)S(1)} %join.1.refs_0_._), custom_call_target="tpu_custom_call" | custom-call | bytes 9437184 | tf_op jit(solution)/shard_map/fetch/pallas_call | solution.py:135
  12.2 2.5 %encode.4 = (bf16[32,2048]{1,0:T(8,128)(2,1)S(1)}, bf16[1152,2048]{1,0:T(8,128)(2,1)S(1)}) custom-call(s32[1]{0:T(128)} %bitcast.me_ref, bf16[32,1152]{1,0:T(8,128)(2,1)S(1)} %get-tuple-element.49.x_ref, bf16[1152,2048]{1,0:T(8,128)(2,1)S(1)} %get-tuple-element.47.here_ref, bf16[1152,8192]{1,0:T(8,128)(2,1)} %refs_0_.3), custom_call_target="tpu_custom_call" | custom-call | flops 150994944 | bytes 4718592 | tf_op jit(solution)/shard_map/encode/pallas_call | solution.py:172
  14.7 2.5 %collective-permute-start.4 = (bf16[32,2048]{1,0:T(8,128)(2,1)S(1)}, bf16[32,2048]{1,0:T(8,128)(2,1)S(1)}, u32[]{:S(2)}, u32[]{:S(2)}) collective-permute-start(bf16[32,2048]{1,0:T(8,128)(2,1)S(1)} %get-tuple-element.48), channel_id=1, source_target_pairs={{0,3},{1,2},{2,1},{3,0},{4,7},{5,6},{6,5},{7,4},{8,11},{9,10},{10,... | collective-permute-start | bytes 393224 | tf_op jit(solution)/shard_map/ppermute | solution.py:42
  17.2 1.3 %encode.7 = bf16[32,2048]{1,0:T(8,128)(2,1)S(1)} custom-call(s32[1]{0:T(128)} %bitcast.me_ref, bf16[32,1152]{1,0:T(8,128)(2,1)S(1)} %get-tuple-element.49.x_ref, bf16[1152,2048]{1,0:T(8,128)(2,1)S(1)} %get-tuple-element.53.here_ref), custom_call_target="tpu_custom_call" | custom-call | flops 150994944 | bytes 4718592 | tf_op jit(solution)/shard_map/encode/pallas_call | solution.py:172
  18.5 2.5 %encode.5 = (bf16[32,2048]{1,0:T(8,128)(2,1)S(1)}, bf16[1152,2048]{1,0:T(8,128)(2,1)S(1)}) custom-call(s32[1]{0:T(128)} %bitcast.me_ref, bf16[32,1152]{1,0:T(8,128)(2,1)S(1)} %get-tuple-element.49.x_ref, bf16[1152,2048]{1,0:T(8,128)(2,1)S(1)} %get-tuple-element.50.here_ref, bf16[1152,8192]{1,0:T(8,128)(2,1)} %refs_0_.3), custom_call_target="tpu_custom_call" | custom-call | flops 150994944 | bytes 4718592 | tf_op jit(solution)/shard_map/encode/pallas_call | solution.py:172
  21.6 1.0 %collective-permute-start.6 = (bf16[32,2048]{1,0:T(8,128)(2,1)S(1)}, bf16[32,2048]{1,0:T(8,128)(2,1)S(1)}, u32[]{:S(2)}, u32[]{:S(2)}) collective-permute-start(bf16[32,2048]{1,0:T(8,128)(2,1)S(1)} %encode.7), channel_id=1, source_target_pairs={{0,2},{1,3},{2,0},{3,1},{4,6},{5,7},{6,4},{7,5},{8,10},{9,11},{10,... | collective-permute-start | bytes 393224 | tf_op jit(solution)/shard_map/ppermute | solution.py:42
  22.7 1.3 %encode.6._.refs_0_ = bf16[32,2048]{1,0:T(8,128)(2,1)S(1)} custom-call(s32[1]{0:T(128)} %bitcast.me_ref, bf16[32,1152]{1,0:T(8,128)(2,1)S(1)} %get-tuple-element.49.x_ref, bf16[1152,2048]{1,0:T(8,128)(2,1)S(1)} %get-tuple-element.51.here_ref), custom_call_target="tpu_custom_call" | custom-call | flops 150994944 | bytes 4718592 | tf_op jit(solution)/shard_map/encode/pallas_call | solution.py:172
  24.0 4.3 %squares.1.a_ref = f32[8,1024]{1,0:T(8,128)S(1)} custom-call(bf16[8192,1152]{1,0:T(8,128)(2,1)S(1)} %bitcast.3, bf16[32,2048]{1,0:T(8,128)(2,1)S(1)} %encode.6._.refs_0_), custom_call_target="tpu_custom_call" | custom-call | flops 18874368 | bytes 18874368 | tf_op jit(solution)/shard_map/squares/pallas_call | solution.py:220
  28.4 2.0 %collective-permute-start.9 = (bf16[32,2048]{1,0:T(8,128)(2,1)S(1)}, bf16[32,2048]{1,0:T(8,128)(2,1)S(1)}, u32[]{:S(2)}, u32[]{:S(2)}) collective-permute-start(bf16[32,2048]{1,0:T(8,128)(2,1)S(1)} %activate.1.act_ref.refs_0_), channel_id=1, source_target_pairs={{0,3},{1,2},{2,1},{3,0},{4,7},{5,6},{6,5},{7,4},{8,11},{9,10},{10,... | collective-permute-start | bytes 393224 | tf_op jit(solution)/shard_map/ppermute | solution.py:42
  30.9 1.1 %collective-permute-start.7 = (bf16[32,2048]{1,0:T(8,128)(2,1)S(1)}, bf16[32,2048]{1,0:T(8,128)(2,1)S(1)}, u32[]{:S(2)}, u32[]{:S(2)}) collective-permute-start(bf16[32,2048]{1,0:T(8,128)(2,1)S(1)} %activate.1.act_ref.refs_0_), channel_id=1, source_target_pairs={{0,1},{1,0},{2,3},{3,2},{4,5},{5,4},{6,7},{7,6},{8,9},{9,8},{10,11... | collective-permute-start | bytes 393224 | tf_op jit(solution)/shard_map/ppermute | solution.py:42
  32.0 1.0 %collective-permute-start.10 = (f32[8,1024]{1,0:T(8,128)S(1)}, f32[8,1024]{1,0:T(8,128)S(1)}, u32[]{:S(2)}, u32[]{:S(2)}) collective-permute-start(f32[8,1024]{1,0:T(8,128)S(1)} %squares.1.a_ref), channel_id=1, source_target_pairs={{0,1},{1,0},{2,3},{3,2},{4,5},{5,4},{6,7},{7,6},{8,9},{9,8},{10,11... | collective-permute-start | bytes 98312 | tf_op jit(solution)/shard_map/ppermute | solution.py:42
  32.9 1.0 %rebuild_own.1.part_ref = f32[32,1152]{1,0:T(8,128)S(1)} custom-call(s32[1]{0:T(128)} %bitcast.me_ref, bf16[32,2048]{1,0:T(8,128)(2,1)S(1)} %activate.1.act_ref.refs_0_, bf16[8192,1152]{1,0:T(8,128)(2,1)S(1)} %bitcast.3), custom_call_target="tpu_custom_call" | custom-call | flops 150994944 | bytes 4718592 | tf_op jit(solution)/shard_map/rebuild_own/pallas_call | solution.py:267
  34.0 2.6 %collective-permute-done.10.b_ref = f32[8,1024]{1,0:T(8,128)S(1)} collective-permute-done((f32[8,1024]{1,0:T(8,128)S(1)}, f32[8,1024]{1,0:T(8,128)S(1)}, u32[]{:S(2)}, u32[]{:S(2)}) %collective-permute-start.10) | collective-permute-done | bytes 32800 | tf_op jit(solution)/shard_map/ppermute | solution.py:42
  36.6 3.3 %rebuild.1 = (f32[32,1152]{1,0:T(8,128)S(1)}, bf16[32,8192]{1,0:T(8,128)(2,1)S(1)}, f32[8,1024]{1,0:T(8,128)S(1)}) custom-call(s32[1]{0:T(128)} %bitcast.me_ref, f32[32,1152]{1,0:T(8,128)S(1)} %rebuild_own.1.part_ref, bf16[32,2048]{1,0:T(8,128)(2,1)S(1)} %activate.1.act_ref.refs_0_, bf16[32,2048]{1,0:T(8,128)(2,1)S(1)} %collective-permute-done.7.refs_1_, ...), custom_call_target="tpu_custom_call" | custom-call | flops 603979776 | bytes 18874368 | tf_op jit(solution)/shard_map/rebuild/pallas_call | solution.py:280
  40.0 1.4 %collective-permute-done.11.other_ref = f32[32,1152]{1,0:T(8,128)S(1)} collective-permute-done((f32[32,1152]{1,0:T(8,128)S(1)}, f32[32,1152]{1,0:T(8,128)S(1)}, u32[]{:S(2)}, u32[]{:S(2)}) %collective-permute-start.11) | collective-permute-done | bytes 147488 | tf_op jit(solution)/shard_map/ppermute | solution.py:42
  41.4 3.5 %collective-permute-start.14 = (bf16[32,1152]{1,0:T(8,128)(2,1)S(1)}, bf16[32,1152]{1,0:T(8,128)(2,1)S(1)}, u32[]{:S(2)}, u32[]{:S(2)}) collective-permute-start(bf16[32,1152]{1,0:T(8,128)(2,1)S(1)} %get-tuple-element.68._), channel_id=1, source_target_pairs={{0,24},{4,28},{8,16},{12,20},{16,8},{20,12},{24,0},{28,4},{1,25},{... | collective-permute-start | bytes 221192 | tf_op jit(solution)/shard_map/ppermute | solution.py:42
  45.0 0.9 %collective-permute-start.12 = (bf16[32,1152]{1,0:T(8,128)(2,1)S(1)}, bf16[32,1152]{1,0:T(8,128)(2,1)S(1)}, u32[]{:S(2)}, u32[]{:S(2)}) collective-permute-start(bf16[32,1152]{1,0:T(8,128)(2,1)S(1)} %get-tuple-element.68._), channel_id=1, source_target_pairs={{0,8},{4,12},{8,0},{12,4},{16,24},{20,28},{24,16},{28,20},{1,9},{5... | collective-permute-start | bytes 221192 | tf_op jit(solution)/shard_map/ppermute | solution.py:42
  45.9 1.5 %collective-permute-start.15 = (f32[8,1024]{1,0:T(8,128)S(1)}, f32[8,1024]{1,0:T(8,128)S(1)}, u32[]{:S(2)}, u32[]{:S(2)}) collective-permute-start(f32[8,1024]{1,0:T(8,128)S(1)} %add.5.s0), channel_id=1, source_target_pairs={{0,2},{1,3},{2,0},{3,1},{4,6},{5,7},{6,4},{7,5},{8,10},{9,11},{10,... | collective-permute-start | bytes 98312 | tf_op jit(solution)/shard_map/ppermute | solution.py:42
  47.4 3.8 %fill.1 = (bf16[2048,1152]{1,0:T(8,128)(2,1)S(1)}, bf16[2048,1152]{1,0:T(8,128)(2,1)S(1)}) custom-call(bf16[8192,1152]{1,0:T(8,128)(2,1)} %m_hbm.3, bf16[8192,1152]{1,0:T(8,128)(2,1)} %v_hbm.3, bf16[32,1152]{1,0:T(8,128)(2,1)S(1)} %get-tuple-element.68._), custom_call_target="tpu_custom_call" | custom-call | bytes 9437184 | tf_op jit(solution)/shard_map/fill/pallas_call | solution.py:440
  51.4 21.2 %adam.1 = (bf16[4,1152]{1,0:T(4,128)(2,1)}, bf16[8192,1152]{1,0:T(8,128)(2,1)}) custom-call(f32[32,1152]{1,0:T(8,128)S(1)} %get-tuple-element.42.acts_ref, f32[32,1152]{1,0:T(8,128)S(1)} %get-tuple-element.67.mine_ref, bf16[32,1152]{1,0:T(8,128)(2,1)S(1)} %collective-permute-done.12.o1, bf16[32,1152]{1,0:T(8,128)(2,1)S(1)} %collective-permute-done.13.o2, ...), custom_call_target="tpu_custom_call" | custom-call | flops 2415919104 | bytes 56623104 | tf_op jit(solution)/shard_map/adam/pallas_call | solution.py:460
  (51 shorter events, 2.6 us)
Async XLA Ops:
  0.6 1.9 %collective-permute-start = (bf16[4,1152]{1,0:T(4,128)(2,1)}, bf16[4,1152]{1,0:T(4,128)(2,1)S(1)}, u32[]{:S(2)}, u32[]{:S(2)}) collective-permute-start(bf16[4,1152]{1,0:T(4,128)(2,1)} %x_ref.1), channel_id=1, source_target_pairs={{0,4},{4,0},{8,12},{12,8},{16,20},{20,16},{24,28},{28,24},{1,5},{5... | collective-permute-start | bytes 27656 | tf_op jit(solution)/shard_map/ppermute | solution.py:42
  2.6 9.1 %collective-permute-start.3 = (f32[8,1152]{1,0:T(8,128)S(1)}, f32[8,1152]{1,0:T(8,128)S(1)}, u32[]{:S(2)}, u32[]{:S(2)}) collective-permute-start(f32[8,1152]{1,0:T(8,128)S(1)} %join.1.refs_0_._), channel_id=1, source_target_pairs={{0,24},{4,28},{8,16},{12,20},{16,8},{20,12},{24,0},{28,4},{1,25},{... | collective-permute-start | bytes 110600 | tf_op jit(solution)/shard_map/ppermute | solution.py:42
  7.2 4.9 %collective-permute-start.2 = (f32[8,1152]{1,0:T(8,128)S(1)}, f32[8,1152]{1,0:T(8,128)S(1)}, u32[]{:S(2)}, u32[]{:S(2)}) collective-permute-start(f32[8,1152]{1,0:T(8,128)S(1)} %join.1.refs_0_._), channel_id=1, source_target_pairs={{0,16},{4,20},{8,24},{12,28},{16,0},{20,4},{24,8},{28,12},{1,17},{... | collective-permute-start | bytes 110600 | tf_op jit(solution)/shard_map/ppermute | solution.py:42
  7.2 4.9 %collective-permute-start.1 = (f32[8,1152]{1,0:T(8,128)S(1)}, f32[8,1152]{1,0:T(8,128)S(1)}, u32[]{:S(2)}, u32[]{:S(2)}) collective-permute-start(f32[8,1152]{1,0:T(8,128)S(1)} %join.1.refs_0_._), channel_id=1, source_target_pairs={{0,8},{4,12},{8,0},{12,4},{16,24},{20,28},{24,16},{28,20},{1,9},{5... | collective-permute-start | bytes 110600 | tf_op jit(solution)/shard_map/ppermute | solution.py:42
  12.1 11.8 %slice-start = ((s8[18874368]{0:T(1024)(128)(4,1)}), s8[4194304]{0:T(1024)(128)(4,1)S(1)}, s32[]{:S(2)}) async-start(s8[18874368]{0:T(1024)(128)(4,1)} %bitcast.2), calls=%async_computation | async-start | bytes 8388608
  12.1 11.8 %slice-start.1 = ((s8[18874368]{0:T(1024)(128)(4,1)}), s8[4194304]{0:T(1024)(128)(4,1)S(1)}, s32[]{:S(2)}) async-start(s8[18874368]{0:T(1024)(128)(4,1)} %bitcast.2), calls=%async_computation.1 | async-start | bytes 8388608
  12.2 11.8 %slice-start.2 = ((s8[18874368]{0:T(1024)(128)(4,1)}), s8[4194304]{0:T(1024)(128)(4,1)S(1)}, s32[]{:S(2)}) async-start(s8[18874368]{0:T(1024)(128)(4,1)} %bitcast.2), calls=%async_computation.2 | async-start | bytes 8388608
  14.7 8.0 %collective-permute-start.4 = (bf16[32,2048]{1,0:T(8,128)(2,1)S(1)}, bf16[32,2048]{1,0:T(8,128)(2,1)S(1)}, u32[]{:S(2)}, u32[]{:S(2)}) collective-permute-start(bf16[32,2048]{1,0:T(8,128)(2,1)S(1)} %get-tuple-element.48), channel_id=1, source_target_pairs={{0,3},{1,2},{2,1},{3,0},{4,7},{5,6},{6,5},{7,4},{8,11},{9,10},{10,... | collective-permute-start | bytes 393224 | tf_op jit(solution)/shard_map/ppermute | solution.py:42
  21.0 7.3 %collective-permute-start.5 = (bf16[32,2048]{1,0:T(8,128)(2,1)S(1)}, bf16[32,2048]{1,0:T(8,128)(2,1)S(1)}, u32[]{:S(2)}, u32[]{:S(2)}) collective-permute-start(bf16[32,2048]{1,0:T(8,128)(2,1)S(1)} %get-tuple-element.52), channel_id=1, source_target_pairs={{0,1},{1,0},{2,3},{3,2},{4,5},{5,4},{6,7},{7,6},{8,9},{9,8},{10,11... | collective-permute-start | bytes 393224 | tf_op jit(solution)/shard_map/ppermute | solution.py:42
  21.6 6.7 %collective-permute-start.6 = (bf16[32,2048]{1,0:T(8,128)(2,1)S(1)}, bf16[32,2048]{1,0:T(8,128)(2,1)S(1)}, u32[]{:S(2)}, u32[]{:S(2)}) collective-permute-start(bf16[32,2048]{1,0:T(8,128)(2,1)S(1)} %encode.7), channel_id=1, source_target_pairs={{0,2},{1,3},{2,0},{3,1},{4,6},{5,7},{6,4},{7,5},{8,10},{9,11},{10,... | collective-permute-start | bytes 393224 | tf_op jit(solution)/shard_map/ppermute | solution.py:42
  28.4 8.2 %collective-permute-start.9 = (bf16[32,2048]{1,0:T(8,128)(2,1)S(1)}, bf16[32,2048]{1,0:T(8,128)(2,1)S(1)}, u32[]{:S(2)}, u32[]{:S(2)}) collective-permute-start(bf16[32,2048]{1,0:T(8,128)(2,1)S(1)} %activate.1.act_ref.refs_0_), channel_id=1, source_target_pairs={{0,3},{1,2},{2,1},{3,0},{4,7},{5,6},{6,5},{7,4},{8,11},{9,10},{10,... | collective-permute-start | bytes 393224 | tf_op jit(solution)/shard_map/ppermute | solution.py:42
  30.4 6.2 %collective-permute-start.8 = (bf16[32,2048]{1,0:T(8,128)(2,1)S(1)}, bf16[32,2048]{1,0:T(8,128)(2,1)S(1)}, u32[]{:S(2)}, u32[]{:S(2)}) collective-permute-start(bf16[32,2048]{1,0:T(8,128)(2,1)S(1)} %activate.1.act_ref.refs_0_), channel_id=1, source_target_pairs={{0,2},{1,3},{2,0},{3,1},{4,6},{5,7},{6,4},{7,5},{8,10},{9,11},{10,... | collective-permute-start | bytes 393224 | tf_op jit(solution)/shard_map/ppermute | solution.py:42
  30.9 5.7 %collective-permute-start.7 = (bf16[32,2048]{1,0:T(8,128)(2,1)S(1)}, bf16[32,2048]{1,0:T(8,128)(2,1)S(1)}, u32[]{:S(2)}, u32[]{:S(2)}) collective-permute-start(bf16[32,2048]{1,0:T(8,128)(2,1)S(1)} %activate.1.act_ref.refs_0_), channel_id=1, source_target_pairs={{0,1},{1,0},{2,3},{3,2},{4,5},{5,4},{6,7},{7,6},{8,9},{9,8},{10,11... | collective-permute-start | bytes 393224 | tf_op jit(solution)/shard_map/ppermute | solution.py:42
  32.0 4.6 %collective-permute-start.10 = (f32[8,1024]{1,0:T(8,128)S(1)}, f32[8,1024]{1,0:T(8,128)S(1)}, u32[]{:S(2)}, u32[]{:S(2)}) collective-permute-start(f32[8,1024]{1,0:T(8,128)S(1)} %squares.1.a_ref), channel_id=1, source_target_pairs={{0,1},{1,0},{2,3},{3,2},{4,5},{5,4},{6,7},{7,6},{8,9},{9,8},{10,11... | collective-permute-start | bytes 98312 | tf_op jit(solution)/shard_map/ppermute | solution.py:42
  39.9 1.4 %collective-permute-start.11 = (f32[32,1152]{1,0:T(8,128)S(1)}, f32[32,1152]{1,0:T(8,128)S(1)}, u32[]{:S(2)}, u32[]{:S(2)}) collective-permute-start(f32[32,1152]{1,0:T(8,128)S(1)} %get-tuple-element.66.mine_ref), channel_id=1, source_target_pairs={{0,4},{4,0},{8,12},{12,8},{16,20},{20,16},{24,28},{28,24},{1,5},{5... | collective-permute-start | bytes 442376 | tf_op jit(solution)/shard_map/ppermute | solution.py:42
  41.4 10.0 %slice-start.5 = ((s8[18874368]{0:T(1024)(128)(4,1)}), s8[4194304]{0:T(1024)(128)(4,1)S(1)}, s32[]{:S(2)}) async-start(s8[18874368]{0:T(1024)(128)(4,1)} %bitcast.4), calls=%async_computation.5 | async-start | bytes 8388608
  41.4 10.0 %slice-start.6 = ((s8[18874368]{0:T(1024)(128)(4,1)}), s8[4194304]{0:T(1024)(128)(4,1)S(1)}, s32[]{:S(2)}) async-start(s8[18874368]{0:T(1024)(128)(4,1)} %bitcast.4), calls=%async_computation.6 | async-start | bytes 8388608
  41.4 10.0 %slice-start.7 = ((s8[18874368]{0:T(1024)(128)(4,1)}), s8[4194304]{0:T(1024)(128)(4,1)S(1)}, s32[]{:S(2)}) async-start(s8[18874368]{0:T(1024)(128)(4,1)} %bitcast.4), calls=%async_computation.7 | async-start | bytes 8388608
  41.4 10.0 %slice-start.8 = ((s8[18874368]{0:T(1024)(128)(4,1)}), s8[4194304]{0:T(1024)(128)(4,1)S(1)}, s32[]{:S(2)}) async-start(s8[18874368]{0:T(1024)(128)(4,1)} %bitcast.4), calls=%async_computation.8 | async-start | bytes 8388608
  41.4 10.0 %slice-start.9 = ((s8[18874368]{0:T(1024)(128)(4,1)}), s8[2097152]{0:T(1024)(128)(4,1)S(1)}, s32[]{:S(2)}) async-start(s8[18874368]{0:T(1024)(128)(4,1)} %bitcast.4), calls=%async_computation.9 | async-start | bytes 4194304
  41.4 9.8 %collective-permute-start.14 = (bf16[32,1152]{1,0:T(8,128)(2,1)S(1)}, bf16[32,1152]{1,0:T(8,128)(2,1)S(1)}, u32[]{:S(2)}, u32[]{:S(2)}) collective-permute-start(bf16[32,1152]{1,0:T(8,128)(2,1)S(1)} %get-tuple-element.68._), channel_id=1, source_target_pairs={{0,24},{4,28},{8,16},{12,20},{16,8},{20,12},{24,0},{28,4},{1,25},{... | collective-permute-start | bytes 221192 | tf_op jit(solution)/shard_map/ppermute | solution.py:42
  44.9 6.5 %collective-permute-start.13 = (bf16[32,1152]{1,0:T(8,128)(2,1)S(1)}, bf16[32,1152]{1,0:T(8,128)(2,1)S(1)}, u32[]{:S(2)}, u32[]{:S(2)}) collective-permute-start(bf16[32,1152]{1,0:T(8,128)(2,1)S(1)} %get-tuple-element.68._), channel_id=1, source_target_pairs={{0,16},{4,20},{8,24},{12,28},{16,0},{20,4},{24,8},{28,12},{1,17},{... | collective-permute-start | bytes 221192 | tf_op jit(solution)/shard_map/ppermute | solution.py:42
  45.0 6.5 %collective-permute-start.12 = (bf16[32,1152]{1,0:T(8,128)(2,1)S(1)}, bf16[32,1152]{1,0:T(8,128)(2,1)S(1)}, u32[]{:S(2)}, u32[]{:S(2)}) collective-permute-start(bf16[32,1152]{1,0:T(8,128)(2,1)S(1)} %get-tuple-element.68._), channel_id=1, source_target_pairs={{0,8},{4,12},{8,0},{12,4},{16,24},{20,28},{24,16},{28,20},{1,9},{5... | collective-permute-start | bytes 221192 | tf_op jit(solution)/shard_map/ppermute | solution.py:42
  45.9 5.3 %collective-permute-start.15 = (f32[8,1024]{1,0:T(8,128)S(1)}, f32[8,1024]{1,0:T(8,128)S(1)}, u32[]{:S(2)}, u32[]{:S(2)}) collective-permute-start(f32[8,1024]{1,0:T(8,128)S(1)} %add.5.s0), channel_id=1, source_target_pairs={{0,2},{1,3},{2,0},{3,1},{4,6},{5,7},{6,4},{7,5},{8,10},{9,11},{10,... | collective-permute-start | bytes 98312 | tf_op jit(solution)/shard_map/ppermute | solution.py:42
  (4 other events, 16.1 us)

commit v4 on v3

--- a/solution.py
+++ b/solution.py
@@ -19,6 +19,7 @@
 bf16 = jnp.bfloat16
 MIB = 1 << 20
 TALL = 1024
+EARLY = 2
 PARTS = ("row", "rep")
 VM = pl.BlockSpec(memory_space=pltpu.VMEM)
 HBM = pl.BlockSpec(memory_space=pltpu.HBM)
@@ -241,11 +242,13 @@
     return lax.fori_loop(0, chunk // tall, body, total)
 
 
-def rebuild_own_kernel(me_ref, act_ref, w_ref, out_ref):
-    out_ref[...] = rebuild_part(0, me_ref, act_ref, w_ref, jnp.zeros(out_ref.shape, f32))
-
-
-def rebuild_kernel(me_ref, part_ref, *refs):
+def rebuild_one_kernel(k, me_ref, act_ref, w_ref, *refs):
+    out_ref = refs[-1]
+    total = refs[0][...] if len(refs) > 1 else jnp.zeros(out_ref.shape, f32)
+    out_ref[...] = rebuild_part(k, me_ref, act_ref, w_ref, total)
+
+
+def rebuild_kernel(ks, me_ref, part_ref, *refs):
     acts, w_ref, (out_ref, all_ref, counts_ref) = refs[:-4], refs[-4], refs[-3:]
     chunk = acts[0].shape[1]
     total = part_ref[...]
@@ -257,28 +260,28 @@
             counts_ref[pl.ds(row, 1), :] = jnp.sum(
                 act[:, c:c + TALL].astype(f32), axis=0, keepdims=True
             )
-        if k:
+        if k in ks:
             total = rebuild_part(k, me_ref, act, w_ref, total)
     out_ref[...] = total
 
 
-def rebuild_own(me, act, w):
+def rebuild_one(k, me, act, w, *part):
     (total, chunk), depth = act.shape, w.shape[1]
     return pl.pallas_call(
-        rebuild_own_kernel,
-        in_specs=[pl.BlockSpec(memory_space=pltpu.SMEM), VM, VM],
+        functools.partial(rebuild_one_kernel, k),
+        in_specs=[pl.BlockSpec(memory_space=pltpu.SMEM), VM, VM] + [VM] * len(part),
         out_specs=VM,
         out_shape=jax.ShapeDtypeStruct((total, depth), f32),
         compiler_params=params(4),
         cost_estimate=cost(2 * total * chunk * depth, 2 * chunk * depth),
-        name="rebuild_own",
-    )(me, act, w)
-
-
-def rebuild(me, part, acts, w):
+        name="rebuild_one",
+    )(me, act, w, *part)
+
+
+def rebuild(ks, me, part, acts, w):
     total, (width, depth) = acts[0].shape[0], w.shape
     return pl.pallas_call(
-        rebuild_kernel,
+        functools.partial(rebuild_kernel, ks),
         in_specs=[pl.BlockSpec(memory_space=pltpu.SMEM)] + [VM] * (len(acts) + 2),
         out_specs=[VM] * 3,
         out_shape=[
@@ -512,10 +515,14 @@
     act = activate(me, enc_bias.reshape(1, -1), arrived)
     act, sums = lax.optimization_barrier((act, sums))
     acts = [act] + [swap(act, PARTS, parts, k) for k in range(1, parts)]
-    sums = add(sums, swap(sums, PARTS, parts, 1))
-    part = rebuild_own(me, act, w)
+    more = swap(sums, PARTS, parts, 1)
+    part = rebuild_one(0, me, act, w)
+    part = rebuild_one(EARLY, me, acts[EARLY], w, part)
+    part, more = lax.optimization_barrier((part, more))
+    sums = add(sums, more)
     acts, sums = lax.optimization_barrier((acts, sums))
-    part, all_act, counts = rebuild(me, part, acts, w)
+    rest = [k for k in range(1, parts) if k != EARLY]
+    part, all_act, counts = rebuild(rest, me, part, acts, w)
     part, narrow = pair_sum(part, swap(part, "feat", feat, 1))
     others = [swap(narrow, "feat", feat, k) for k in (2, 4, 6)]
     sums = (sums, swap(sums, PARTS, parts, 2))

time: 72.9 us -> 72.7 us (level)
    pallas_call x2 -> x3, Pallas kernels: 4.33 us -> 4.33 us  [the longest x1 2.24 us: rebuild(): pl.pallas_call(functools.partial(rebuild_kernel, ks), in_specs=[pl.BlockS...]
  transfers between devices with their start and end apart: 16 -> 16, of which waited for: 4 -> 5; matrix products, arithmetic and copies ran while one was open for 1% -> 1% of each run, Pallas kernels for 25% -> 26%
where the time goes in v4:
time: 72.7 us; the launch traced here: 72.4 us
  Pallas kernels  45.1 us (62%)
  starting transfers between devices  19.9 us (27%)
  waiting for transfers between devices  4.95 us (7%)
  local copies, waits for them, and re-layouts  1.5 us (2%)
  between operations  0.94 us (1%)
    pallas_call x1, Pallas kernels, adam(): pl.pallas_call(functools.partial(adam_kernel, tall, block), in_specs=[VM]...  21.2 us
    ppermute x16, starting transfers between devices, swap(): return lax.ppermute(x, axis, [(a, a ^ k) for a in range(n)])  19.9 us
    pallas_call x4, Pallas kernels, encode(): pl.pallas_call(functools.partial(encode_kernel, ahead), in_specs=[pl.Bloc...  7.58 us
    ppermute x16, waiting for transfers between devices, swap(): return lax.ppermute(x, axis, [(a, a ^ k) for a in range(n)])  4.95 us
    pallas_call x1, Pallas kernels, squares(): pl.pallas_call(squares_kernel, in_specs=[VM, ANY], out_specs=VM, out_shap...  4.26 us
    pallas_call x1, Pallas kernels, fill(): pl.pallas_call(fill_kernel, in_specs=[HBM, HBM, ANY], out_specs=[VM, VM],...  3.83 us
    pallas_call x1, Pallas kernels, fetch(): pl.pallas_call(functools.partial(fetch_kernel, ks), in_specs=[pl.BlockSpe...  3.8 us
    pallas_call x1, Pallas kernels, rebuild(): pl.pallas_call(functools.partial(rebuild_kernel, ks), in_specs=[pl.BlockS...  2.24 us
  transfers between devices with their start and end apart: 16, of which 5 were waited for; matrix products, arithmetic and copies ran while one was open for 1% of the time, Pallas kernels for 26%

profile of v4, /device:TPU:0, one launch (start us, length us, event | category | flops | bytes accessed | tf_op | source)
XLA Modules:
  0.0 72.4 jit_solution(9471536138651558050)
XLA Ops:
  2.6 4.7 %collective-permute-start.3 = (f32[8,1152]{1,0:T(8,128)S(1)}, f32[8,1152]{1,0:T(8,128)S(1)}, u32[]{:S(2)}, u32[]{:S(2)}) collective-permute-start(f32[8,1152]{1,0:T(8,128)S(1)} %join.1.refs_0_._), channel_id=1, source_target_pairs={{0,24},{4,28},{8,16},{12,20},{16,8},{20,12},{24,0},{28,4},{1,25},{... | collective-permute-start | bytes 110600 | tf_op jit(solution)/shard_map/ppermute | solution.py:43
  7.9 3.8 %fetch.1 = (bf16[1152,2048]{1,0:T(8,128)(2,1)S(1)}, bf16[1152,2048]{1,0:T(8,128)(2,1)S(1)}) custom-call(s32[1]{0:T(128)} %bitcast.me_ref, bf16[1152,8192]{1,0:T(8,128)(2,1)} %refs_0_.3, f32[8,1152]{1,0:T(8,128)S(1)} %join.1.refs_0_._), custom_call_target="tpu_custom_call" | custom-call | bytes 9437184 | tf_op jit(solution)/shard_map/fetch/pallas_call | solution.py:136
  12.2 2.5 %encode.4 = (bf16[32,2048]{1,0:T(8,128)(2,1)S(1)}, bf16[1152,2048]{1,0:T(8,128)(2,1)S(1)}) custom-call(s32[1]{0:T(128)} %bitcast.me_ref, bf16[32,1152]{1,0:T(8,128)(2,1)S(1)} %get-tuple-element.51.x_ref, bf16[1152,2048]{1,0:T(8,128)(2,1)S(1)} %get-tuple-element.49.here_ref, bf16[1152,8192]{1,0:T(8,128)(2,1)} %refs_0_.3), custom_call_target="tpu_custom_call" | custom-call | flops 150994944 | bytes 4718592 | tf_op jit(solution)/shard_map/encode/pallas_call | solution.py:173
  14.7 2.5 %collective-permute-start.4 = (bf16[32,2048]{1,0:T(8,128)(2,1)S(1)}, bf16[32,2048]{1,0:T(8,128)(2,1)S(1)}, u32[]{:S(2)}, u32[]{:S(2)}) collective-permute-start(bf16[32,2048]{1,0:T(8,128)(2,1)S(1)} %get-tuple-element.50), channel_id=1, source_target_pairs={{0,3},{1,2},{2,1},{3,0},{4,7},{5,6},{6,5},{7,4},{8,11},{9,10},{10,... | collective-permute-start | bytes 393224 | tf_op jit(solution)/shard_map/ppermute | solution.py:43
  17.2 1.3 %encode.7 = bf16[32,2048]{1,0:T(8,128)(2,1)S(1)} custom-call(s32[1]{0:T(128)} %bitcast.me_ref, bf16[32,1152]{1,0:T(8,128)(2,1)S(1)} %get-tuple-element.51.x_ref, bf16[1152,2048]{1,0:T(8,128)(2,1)S(1)} %get-tuple-element.55.here_ref), custom_call_target="tpu_custom_call" | custom-call | flops 150994944 | bytes 4718592 | tf_op jit(solution)/shard_map/encode/pallas_call | solution.py:173
  18.5 2.5 %encode.5 = (bf16[32,2048]{1,0:T(8,128)(2,1)S(1)}, bf16[1152,2048]{1,0:T(8,128)(2,1)S(1)}) custom-call(s32[1]{0:T(128)} %bitcast.me_ref, bf16[32,1152]{1,0:T(8,128)(2,1)S(1)} %get-tuple-element.51.x_ref, bf16[1152,2048]{1,0:T(8,128)(2,1)S(1)} %get-tuple-element.52.here_ref, bf16[1152,8192]{1,0:T(8,128)(2,1)} %refs_0_.3), custom_call_target="tpu_custom_call" | custom-call | flops 150994944 | bytes 4718592 | tf_op jit(solution)/shard_map/encode/pallas_call | solution.py:173
  21.6 1.0 %collective-permute-start.6 = (bf16[32,2048]{1,0:T(8,128)(2,1)S(1)}, bf16[32,2048]{1,0:T(8,128)(2,1)S(1)}, u32[]{:S(2)}, u32[]{:S(2)}) collective-permute-start(bf16[32,2048]{1,0:T(8,128)(2,1)S(1)} %encode.7), channel_id=1, source_target_pairs={{0,2},{1,3},{2,0},{3,1},{4,6},{5,7},{6,4},{7,5},{8,10},{9,11},{10,... | collective-permute-start | bytes 393224 | tf_op jit(solution)/shard_map/ppermute | solution.py:43
  22.7 1.3 %encode.6._.refs_0_ = bf16[32,2048]{1,0:T(8,128)(2,1)S(1)} custom-call(s32[1]{0:T(128)} %bitcast.me_ref, bf16[32,1152]{1,0:T(8,128)(2,1)S(1)} %get-tuple-element.51.x_ref, bf16[1152,2048]{1,0:T(8,128)(2,1)S(1)} %get-tuple-element.53.here_ref), custom_call_target="tpu_custom_call" | custom-call | flops 150994944 | bytes 4718592 | tf_op jit(solution)/shard_map/encode/pallas_call | solution.py:173
  24.0 4.3 %squares.1.a_ref = f32[8,1024]{1,0:T(8,128)S(1)} custom-call(bf16[8192,1152]{1,0:T(8,128)(2,1)S(1)} %bitcast.3, bf16[32,2048]{1,0:T(8,128)(2,1)S(1)} %encode.6._.refs_0_), custom_call_target="tpu_custom_call" | custom-call | flops 18874368 | bytes 18874368 | tf_op jit(solution)/shard_map/squares/pallas_call | solution.py:221
  28.4 1.1 %collective-permute-start.7 = (bf16[32,2048]{1,0:T(8,128)(2,1)S(1)}, bf16[32,2048]{1,0:T(8,128)(2,1)S(1)}, u32[]{:S(2)}, u32[]{:S(2)}) collective-permute-start(bf16[32,2048]{1,0:T(8,128)(2,1)S(1)} %activate.1.act_ref.refs_0_), channel_id=1, source_target_pairs={{0,2},{1,3},{2,0},{3,1},{4,6},{5,7},{6,4},{7,5},{8,10},{9,11},{10,... | collective-permute-start | bytes 393224 | tf_op jit(solution)/shard_map/ppermute | solution.py:43
  29.5 1.4 %collective-permute-start.10 = (bf16[32,2048]{1,0:T(8,128)(2,1)S(1)}, bf16[32,2048]{1,0:T(8,128)(2,1)S(1)}, u32[]{:S(2)}, u32[]{:S(2)}) collective-permute-start(bf16[32,2048]{1,0:T(8,128)(2,1)S(1)} %activate.1.act_ref.refs_0_), channel_id=1, source_target_pairs={{0,3},{1,2},{2,1},{3,0},{4,7},{5,6},{6,5},{7,4},{8,11},{9,10},{10,... | collective-permute-start | bytes 393224 | tf_op jit(solution)/shard_map/ppermute | solution.py:43
  30.9 1.1 %collective-permute-start.9 = (bf16[32,2048]{1,0:T(8,128)(2,1)S(1)}, bf16[32,2048]{1,0:T(8,128)(2,1)S(1)}, u32[]{:S(2)}, u32[]{:S(2)}) collective-permute-start(bf16[32,2048]{1,0:T(8,128)(2,1)S(1)} %activate.1.act_ref.refs_0_), channel_id=1, source_target_pairs={{0,1},{1,0},{2,3},{3,2},{4,5},{5,4},{6,7},{7,6},{8,9},{9,8},{10,11... | collective-permute-start | bytes 393224 | tf_op jit(solution)/shard_map/ppermute | solution.py:43
  32.0 1.0 %collective-permute-start.8 = (f32[8,1024]{1,0:T(8,128)S(1)}, f32[8,1024]{1,0:T(8,128)S(1)}, u32[]{:S(2)}, u32[]{:S(2)}) collective-permute-start(f32[8,1024]{1,0:T(8,128)S(1)} %squares.1.a_ref), channel_id=1, source_target_pairs={{0,1},{1,0},{2,3},{3,2},{4,5},{5,4},{6,7},{7,6},{8,9},{9,8},{10,11... | collective-permute-start | bytes 98312 | tf_op jit(solution)/shard_map/ppermute | solution.py:43
  32.9 1.0 %rebuild_one.2.refs_0_ = f32[32,1152]{1,0:T(8,128)S(1)} custom-call(s32[1]{0:T(128)} %bitcast.me_ref, bf16[32,2048]{1,0:T(8,128)(2,1)S(1)} %activate.1.act_ref.refs_0_, bf16[8192,1152]{1,0:T(8,128)(2,1)S(1)} %bitcast.3), custom_call_target="tpu_custom_call" | custom-call | flops 150994944 | bytes 4718592 | tf_op jit(solution)/shard_map/rebuild_one/pallas_call | solution.py:270
  34.4 1.0 %rebuild_one.3.part_ref = f32[32,1152]{1,0:T(8,128)S(1)} custom-call(s32[1]{0:T(128)} %bitcast.me_ref, bf16[32,2048]{1,0:T(8,128)(2,1)S(1)} %collective-permute-done.7.act_ref.refs_2_, bf16[8192,1152]{1,0:T(8,128)(2,1)S(1)} %bitcast.3, f32[32,1152]{1,0:T(8,128)S(1)} %rebuild_one.2.refs_0_), custom_call_target="tpu_custom_call" | custom-call | flops 150994944 | bytes 4718592 | tf_op jit(solution)/shard_map/rebuild_one/pallas_call | solution.py:270
  35.5 1.9 %collective-permute-done.8.b_ref = f32[8,1024]{1,0:T(8,128)S(1)} collective-permute-done((f32[8,1024]{1,0:T(8,128)S(1)}, f32[8,1024]{1,0:T(8,128)S(1)}, u32[]{:S(2)}, u32[]{:S(2)}) %collective-permute-start.8) | collective-permute-done | bytes 32800 | tf_op jit(solution)/shard_map/ppermute | solution.py:43
  37.4 2.2 %rebuild.1 = (f32[32,1152]{1,0:T(8,128)S(1)}, bf16[32,8192]{1,0:T(8,128)(2,1)S(1)}, f32[8,1024]{1,0:T(8,128)S(1)}) custom-call(s32[1]{0:T(128)} %bitcast.me_ref, f32[32,1152]{1,0:T(8,128)S(1)} %rebuild_one.3.part_ref, bf16[32,2048]{1,0:T(8,128)(2,1)S(1)} %activate.1.act_ref.refs_0_, bf16[32,2048]{1,0:T(8,128)(2,1)S(1)} %collective-permute-done.9.refs_1_, ...), custom_call_target="tpu_custom_call" | custom-call | flops 603979776 | bytes 18874368 | tf_op jit(solution)/shard_map/rebuild/pallas_call | solution.py:283
  39.8 1.4 %collective-permute-done.11.other_ref = f32[32,1152]{1,0:T(8,128)S(1)} collective-permute-done((f32[32,1152]{1,0:T(8,128)S(1)}, f32[32,1152]{1,0:T(8,128)S(1)}, u32[]{:S(2)}, u32[]{:S(2)}) %collective-permute-start.11) | collective-permute-done | bytes 147488 | tf_op jit(solution)/shard_map/ppermute | solution.py:43
  41.2 3.5 %collective-permute-start.14 = (bf16[32,1152]{1,0:T(8,128)(2,1)S(1)}, bf16[32,1152]{1,0:T(8,128)(2,1)S(1)}, u32[]{:S(2)}, u32[]{:S(2)}) collective-permute-start(bf16[32,1152]{1,0:T(8,128)(2,1)S(1)} %get-tuple-element.72._), channel_id=1, source_target_pairs={{0,24},{4,28},{8,16},{12,20},{16,8},{20,12},{24,0},{28,4},{1,25},{... | collective-permute-start | bytes 221192 | tf_op jit(solution)/shard_map/ppermute | solution.py:43
  44.7 0.9 %collective-permute-start.12 = (bf16[32,1152]{1,0:T(8,128)(2,1)S(1)}, bf16[32,1152]{1,0:T(8,128)(2,1)S(1)}, u32[]{:S(2)}, u32[]{:S(2)}) collective-permute-start(bf16[32,1152]{1,0:T(8,128)(2,1)S(1)} %get-tuple-element.72._), channel_id=1, source_target_pairs={{0,8},{4,12},{8,0},{12,4},{16,24},{20,28},{24,16},{28,20},{1,9},{5... | collective-permute-start | bytes 221192 | tf_op jit(solution)/shard_map/ppermute | solution.py:43
  45.7 0.9 %collective-permute-start.15 = (f32[8,1024]{1,0:T(8,128)S(1)}, f32[8,1024]{1,0:T(8,128)S(1)}, u32[]{:S(2)}, u32[]{:S(2)}) collective-permute-start(f32[8,1024]{1,0:T(8,128)S(1)} %add.5.s0), channel_id=1, source_target_pairs={{0,2},{1,3},{2,0},{3,1},{4,6},{5,7},{6,4},{7,5},{8,10},{9,11},{10,... | collective-permute-start | bytes 98312 | tf_op jit(solution)/shard_map/ppermute | solution.py:43
  46.5 3.8 %fill.1 = (bf16[2048,1152]{1,0:T(8,128)(2,1)S(1)}, bf16[2048,1152]{1,0:T(8,128)(2,1)S(1)}) custom-call(bf16[8192,1152]{1,0:T(8,128)(2,1)} %m_hbm.3, bf16[8192,1152]{1,0:T(8,128)(2,1)} %v_hbm.3, bf16[32,1152]{1,0:T(8,128)(2,1)S(1)} %get-tuple-element.72._), custom_call_target="tpu_custom_call" | custom-call | bytes 9437184 | tf_op jit(solution)/shard_map/fill/pallas_call | solution.py:443
  50.4 0.8 %collective-permute-done.13.o2 = bf16[32,1152]{1,0:T(8,128)(2,1)S(1)} collective-permute-done((bf16[32,1152]{1,0:T(8,128)(2,1)S(1)}, bf16[32,1152]{1,0:T(8,128)(2,1)S(1)}, u32[]{:S(2)}, u32[]{:S(2)}) %collective-permute-start.13) | collective-permute-done | bytes 73760 | tf_op jit(solution)/shard_map/ppermute | solution.py:43
  51.2 21.2 %adam.1 = (bf16[4,1152]{1,0:T(4,128)(2,1)}, bf16[8192,1152]{1,0:T(8,128)(2,1)}) custom-call(f32[32,1152]{1,0:T(8,128)S(1)} %get-tuple-element.44.acts_ref, f32[32,1152]{1,0:T(8,128)S(1)} %get-tuple-element.71.mine_ref, bf16[32,1152]{1,0:T(8,128)(2,1)S(1)} %collective-permute-done.12.o1, bf16[32,1152]{1,0:T(8,128)(2,1)S(1)} %collective-permute-done.13.o2, ...), custom_call_target="tpu_custom_call" | custom-call | flops 2415919104 | bytes 56623104 | tf_op jit(solution)/shard_map/adam/pallas_call | solution.py:463
  (52 shorter events, 4.3 us)
Async XLA Ops:
  0.6 1.9 %collective-permute-start = (bf16[4,1152]{1,0:T(4,128)(2,1)}, bf16[4,1152]{1,0:T(4,128)(2,1)S(1)}, u32[]{:S(2)}, u32[]{:S(2)}) collective-permute-start(bf16[4,1152]{1,0:T(4,128)(2,1)} %x_ref.1), channel_id=1, source_target_pairs={{0,4},{4,0},{8,12},{12,8},{16,20},{20,16},{24,28},{28,24},{1,5},{5... | collective-permute-start | bytes 27656 | tf_op jit(solution)/shard_map/ppermute | solution.py:43
  2.6 9.1 %collective-permute-start.3 = (f32[8,1152]{1,0:T(8,128)S(1)}, f32[8,1152]{1,0:T(8,128)S(1)}, u32[]{:S(2)}, u32[]{:S(2)}) collective-permute-start(f32[8,1152]{1,0:T(8,128)S(1)} %join.1.refs_0_._), channel_id=1, source_target_pairs={{0,24},{4,28},{8,16},{12,20},{16,8},{20,12},{24,0},{28,4},{1,25},{... | collective-permute-start | bytes 110600 | tf_op jit(solution)/shard_map/ppermute | solution.py:43
  7.2 4.9 %collective-permute-start.2 = (f32[8,1152]{1,0:T(8,128)S(1)}, f32[8,1152]{1,0:T(8,128)S(1)}, u32[]{:S(2)}, u32[]{:S(2)}) collective-permute-start(f32[8,1152]{1,0:T(8,128)S(1)} %join.1.refs_0_._), channel_id=1, source_target_pairs={{0,16},{4,20},{8,24},{12,28},{16,0},{20,4},{24,8},{28,12},{1,17},{... | collective-permute-start | bytes 110600 | tf_op jit(solution)/shard_map/ppermute | solution.py:43
  7.2 4.9 %collective-permute-start.1 = (f32[8,1152]{1,0:T(8,128)S(1)}, f32[8,1152]{1,0:T(8,128)S(1)}, u32[]{:S(2)}, u32[]{:S(2)}) collective-permute-start(f32[8,1152]{1,0:T(8,128)S(1)} %join.1.refs_0_._), channel_id=1, source_target_pairs={{0,8},{4,12},{8,0},{12,4},{16,24},{20,28},{24,16},{28,20},{1,9},{5... | collective-permute-start | bytes 110600 | tf_op jit(solution)/shard_map/ppermute | solution.py:43
  12.1 11.8 %slice-start = ((s8[18874368]{0:T(1024)(128)(4,1)}), s8[4194304]{0:T(1024)(128)(4,1)S(1)}, s32[]{:S(2)}) async-start(s8[18874368]{0:T(1024)(128)(4,1)} %bitcast.2), calls=%async_computation | async-start | bytes 8388608
  12.1 11.8 %slice-start.1 = ((s8[18874368]{0:T(1024)(128)(4,1)}), s8[4194304]{0:T(1024)(128)(4,1)S(1)}, s32[]{:S(2)}) async-start(s8[18874368]{0:T(1024)(128)(4,1)} %bitcast.2), calls=%async_computation.1 | async-start | bytes 8388608
  12.2 11.8 %slice-start.2 = ((s8[18874368]{0:T(1024)(128)(4,1)}), s8[4194304]{0:T(1024)(128)(4,1)S(1)}, s32[]{:S(2)}) async-start(s8[18874368]{0:T(1024)(128)(4,1)} %bitcast.2), calls=%async_computation.2 | async-start | bytes 8388608
  14.7 8.0 %collective-permute-start.4 = (bf16[32,2048]{1,0:T(8,128)(2,1)S(1)}, bf16[32,2048]{1,0:T(8,128)(2,1)S(1)}, u32[]{:S(2)}, u32[]{:S(2)}) collective-permute-start(bf16[32,2048]{1,0:T(8,128)(2,1)S(1)} %get-tuple-element.50), channel_id=1, source_target_pairs={{0,3},{1,2},{2,1},{3,0},{4,7},{5,6},{6,5},{7,4},{8,11},{9,10},{10,... | collective-permute-start | bytes 393224 | tf_op jit(solution)/shard_map/ppermute | solution.py:43
  21.0 7.3 %collective-permute-start.5 = (bf16[32,2048]{1,0:T(8,128)(2,1)S(1)}, bf16[32,2048]{1,0:T(8,128)(2,1)S(1)}, u32[]{:S(2)}, u32[]{:S(2)}) collective-permute-start(bf16[32,2048]{1,0:T(8,128)(2,1)S(1)} %get-tuple-element.54), channel_id=1, source_target_pairs={{0,1},{1,0},{2,3},{3,2},{4,5},{5,4},{6,7},{7,6},{8,9},{9,8},{10,11... | collective-permute-start | bytes 393224 | tf_op jit(solution)/shard_map/ppermute | solution.py:43
  21.6 6.7 %collective-permute-start.6 = (bf16[32,2048]{1,0:T(8,128)(2,1)S(1)}, bf16[32,2048]{1,0:T(8,128)(2,1)S(1)}, u32[]{:S(2)}, u32[]{:S(2)}) collective-permute-start(bf16[32,2048]{1,0:T(8,128)(2,1)S(1)} %encode.7), channel_id=1, source_target_pairs={{0,2},{1,3},{2,0},{3,1},{4,6},{5,7},{6,4},{7,5},{8,10},{9,11},{10,... | collective-permute-start | bytes 393224 | tf_op jit(solution)/shard_map/ppermute | solution.py:43
  28.4 6.0 %collective-permute-start.7 = (bf16[32,2048]{1,0:T(8,128)(2,1)S(1)}, bf16[32,2048]{1,0:T(8,128)(2,1)S(1)}, u32[]{:S(2)}, u32[]{:S(2)}) collective-permute-start(bf16[32,2048]{1,0:T(8,128)(2,1)S(1)} %activate.1.act_ref.refs_0_), channel_id=1, source_target_pairs={{0,2},{1,3},{2,0},{3,1},{4,6},{5,7},{6,4},{7,5},{8,10},{9,11},{10,... | collective-permute-start | bytes 393224 | tf_op jit(solution)/shard_map/ppermute | solution.py:43
  29.5 7.9 %collective-permute-start.10 = (bf16[32,2048]{1,0:T(8,128)(2,1)S(1)}, bf16[32,2048]{1,0:T(8,128)(2,1)S(1)}, u32[]{:S(2)}, u32[]{:S(2)}) collective-permute-start(bf16[32,2048]{1,0:T(8,128)(2,1)S(1)} %activate.1.act_ref.refs_0_), channel_id=1, source_target_pairs={{0,3},{1,2},{2,1},{3,0},{4,7},{5,6},{6,5},{7,4},{8,11},{9,10},{10,... | collective-permute-start | bytes 393224 | tf_op jit(solution)/shard_map/ppermute | solution.py:43
  30.9 6.5 %collective-permute-start.9 = (bf16[32,2048]{1,0:T(8,128)(2,1)S(1)}, bf16[32,2048]{1,0:T(8,128)(2,1)S(1)}, u32[]{:S(2)}, u32[]{:S(2)}) collective-permute-start(bf16[32,2048]{1,0:T(8,128)(2,1)S(1)} %activate.1.act_ref.refs_0_), channel_id=1, source_target_pairs={{0,1},{1,0},{2,3},{3,2},{4,5},{5,4},{6,7},{7,6},{8,9},{9,8},{10,11... | collective-permute-start | bytes 393224 | tf_op jit(solution)/shard_map/ppermute | solution.py:43
  32.0 5.4 %collective-permute-start.8 = (f32[8,1024]{1,0:T(8,128)S(1)}, f32[8,1024]{1,0:T(8,128)S(1)}, u32[]{:S(2)}, u32[]{:S(2)}) collective-permute-start(f32[8,1024]{1,0:T(8,128)S(1)} %squares.1.a_ref), channel_id=1, source_target_pairs={{0,1},{1,0},{2,3},{3,2},{4,5},{5,4},{6,7},{7,6},{8,9},{9,8},{10,11... | collective-permute-start | bytes 98312 | tf_op jit(solution)/shard_map/ppermute | solution.py:43
  39.7 1.4 %collective-permute-start.11 = (f32[32,1152]{1,0:T(8,128)S(1)}, f32[32,1152]{1,0:T(8,128)S(1)}, u32[]{:S(2)}, u32[]{:S(2)}) collective-permute-start(f32[32,1152]{1,0:T(8,128)S(1)} %get-tuple-element.70.mine_ref), channel_id=1, source_target_pairs={{0,4},{4,0},{8,12},{12,8},{16,20},{20,16},{24,28},{28,24},{1,5},{5... | collective-permute-start | bytes 442376 | tf_op jit(solution)/shard_map/ppermute | solution.py:43
  41.1 10.0 %slice-start.5 = ((s8[18874368]{0:T(1024)(128)(4,1)}), s8[4194304]{0:T(1024)(128)(4,1)S(1)}, s32[]{:S(2)}) async-start(s8[18874368]{0:T(1024)(128)(4,1)} %bitcast.4), calls=%async_computation.5 | async-start | bytes 8388608
  41.2 10.0 %slice-start.6 = ((s8[18874368]{0:T(1024)(128)(4,1)}), s8[4194304]{0:T(1024)(128)(4,1)S(1)}, s32[]{:S(2)}) async-start(s8[18874368]{0:T(1024)(128)(4,1)} %bitcast.4), calls=%async_computation.6 | async-start | bytes 8388608
  41.2 10.0 %slice-start.7 = ((s8[18874368]{0:T(1024)(128)(4,1)}), s8[4194304]{0:T(1024)(128)(4,1)S(1)}, s32[]{:S(2)}) async-start(s8[18874368]{0:T(1024)(128)(4,1)} %bitcast.4), calls=%async_computation.7 | async-start | bytes 8388608
  41.2 10.0 %slice-start.8 = ((s8[18874368]{0:T(1024)(128)(4,1)}), s8[4194304]{0:T(1024)(128)(4,1)S(1)}, s32[]{:S(2)}) async-start(s8[18874368]{0:T(1024)(128)(4,1)} %bitcast.4), calls=%async_computation.8 | async-start | bytes 8388608
  41.2 10.0 %slice-start.9 = ((s8[18874368]{0:T(1024)(128)(4,1)}), s8[2097152]{0:T(1024)(128)(4,1)S(1)}, s32[]{:S(2)}) async-start(s8[18874368]{0:T(1024)(128)(4,1)} %bitcast.4), calls=%async_computation.9 | async-start | bytes 4194304
  41.2 9.2 %collective-permute-start.14 = (bf16[32,1152]{1,0:T(8,128)(2,1)S(1)}, bf16[32,1152]{1,0:T(8,128)(2,1)S(1)}, u32[]{:S(2)}, u32[]{:S(2)}) collective-permute-start(bf16[32,1152]{1,0:T(8,128)(2,1)S(1)} %get-tuple-element.72._), channel_id=1, source_target_pairs={{0,24},{4,28},{8,16},{12,20},{16,8},{20,12},{24,0},{28,4},{1,25},{... | collective-permute-start | bytes 221192 | tf_op jit(solution)/shard_map/ppermute | solution.py:43
  44.7 6.4 %collective-permute-start.13 = (bf16[32,1152]{1,0:T(8,128)(2,1)S(1)}, bf16[32,1152]{1,0:T(8,128)(2,1)S(1)}, u32[]{:S(2)}, u32[]{:S(2)}) collective-permute-start(bf16[32,1152]{1,0:T(8,128)(2,1)S(1)} %get-tuple-element.72._), channel_id=1, source_target_pairs={{0,16},{4,20},{8,24},{12,28},{16,0},{20,4},{24,8},{28,12},{1,17},{... | collective-permute-start | bytes 221192 | tf_op jit(solution)/shard_map/ppermute | solution.py:43
  44.7 6.4 %collective-permute-start.12 = (bf16[32,1152]{1,0:T(8,128)(2,1)S(1)}, bf16[32,1152]{1,0:T(8,128)(2,1)S(1)}, u32[]{:S(2)}, u32[]{:S(2)}) collective-permute-start(bf16[32,1152]{1,0:T(8,128)(2,1)S(1)} %get-tuple-element.72._), channel_id=1, source_target_pairs={{0,8},{4,12},{8,0},{12,4},{16,24},{20,28},{24,16},{28,20},{1,9},{5... | collective-permute-start | bytes 221192 | tf_op jit(solution)/shard_map/ppermute | solution.py:43
  45.7 4.7 %collective-permute-start.15 = (f32[8,1024]{1,0:T(8,128)S(1)}, f32[8,1024]{1,0:T(8,128)S(1)}, u32[]{:S(2)}, u32[]{:S(2)}) collective-permute-start(f32[8,1024]{1,0:T(8,128)S(1)} %add.5.s0), channel_id=1, source_target_pairs={{0,2},{1,3},{2,0},{3,1},{4,6},{5,7},{6,4},{7,5},{8,10},{9,11},{10,... | collective-permute-start | bytes 98312 | tf_op jit(solution)/shard_map/ppermute | solution.py:43
  (4 other events, 16.1 us)
